TPU v7x, 32 devices: a whole 2x2x4 slice. The times are simulated.
32 devices in a mesh: rows: 8 (over z, x), tm: 4 (over y, core).
Axes of the slice: x: 2, y: 2, z: 4, core: 2. Of those that a mesh axis runs over, the one named last changes fastest.
Arguments:
- jacobian: bfloat16 [8, 3072, 512], P('tm', 'rows'), may hold values from -3 to 3
- rhs: bfloat16 [8, 3072], P('tm', 'rows'), may hold values from -6 to 6
- forget: float32 [8], P('tm'), may hold values from 0.99 to 1
- restart: int32 [8], P('tm'), may hold values 0 or 1
Outputs:
- factor: float32 [8, 512, 512], P('tm', 'rows')
- state: float32 [8, 512], P('tm', 'rows')
All inputs are finite; a program needn't handle non-finite values. No bound on the sum of `restart` on one device may be relied on, other than what follows from the above.
Results may differ from a plain program's by a relative error of at most 0.0003.
Values sent between devices are 32-bit elements; how exact they have to be, the bound alone decides.
A program may use at most 128 MiB of HBM per device.

v0:
```python
import jax
import jax.numpy as jnp
from jax import lax
from jax.sharding import PartitionSpec as P


def prefix(value, axis, join, neutral):
    count, mine = (lax.axis_size(axis), lax.axis_index(axis))
    pieces = jax.tree.map(lambda part: lax.all_gather(part, axis), value)
    total = jax.tree.map(
        lambda part, zero: jnp.full_like(part, 0) + jnp.asarray(zero, part.dtype), value, neutral
    )

    def turn(position, total):
        longer = join(total, jax.tree.map(lambda part: part[position], pieces))
        return jax.tree.map(lambda new, old: jnp.where(position < mine, new, old), longer, total)

    return lax.fori_loop(0, count - 1, turn, total)


def chain_join(earlier, later_part):
    return (
        earlier[0] * later_part[0],
        later_part[0] * earlier[1] + later_part[1],
        later_part[0] * earlier[2] + later_part[2],
    )


def running(matrices, vectors, decays):
    matrix_now = jnp.zeros_like(matrices[0])
    vector_now = jnp.zeros_like(vectors[0])
    retained = jnp.float32(1.0)
    local_mats, local_vecs, retain_list = ([], [], [])
    for position in range(len(matrices)):
        matrix_now = decays[position] * matrix_now + matrices[position]
        vector_now = decays[position] * vector_now + vectors[position]
        retained = retained * decays[position]
        local_mats.append(matrix_now)
        local_vecs.append(vector_now)
        retain_list.append(retained)
    return (local_mats, local_vecs, retain_list)


def solve_rows(matrix, vector, row_start, row_share):
    lower_factor = jnp.linalg.cholesky(matrix)
    middle = jax.scipy.linalg.solve_triangular(lower_factor, vector, lower=True)
    result = jax.scipy.linalg.solve_triangular(lower_factor, middle, lower=True, trans=1)
    upper_rows = lax.dynamic_slice_in_dim(lower_factor.T, row_start, row_share, 0)
    result_rows = lax.dynamic_slice_in_dim(result, row_start, row_share, 0)
    return (upper_rows, result_rows)


def on_device(jacobian, rhs, forget, restart):
    segments_here = jacobian.shape[0]
    state_width = jacobian.shape[2]
    row_share = state_width // lax.axis_size("rows")
    row_start = lax.axis_index("rows") * row_share
    decays = forget * (1.0 - 0.2 * restart.astype(jnp.float32))
    partial_value = jnp.einsum(
        "srv,srw->svw", jacobian, jacobian, preferred_element_type=jnp.float32
    )
    gradient = jnp.einsum("sr,srv->sv", rhs, jacobian, preferred_element_type=jnp.float32)
    information, projected = lax.psum((partial_value, gradient), "rows")
    matrices = [information[position] for position in range(segments_here)]
    vectors = [projected[position] for position in range(segments_here)]
    local_mats, local_vecs, retain_list = running(matrices, vectors, decays)
    identity = (jnp.float32(1.0), jnp.zeros_like(local_mats[0]), jnp.zeros_like(local_vecs[0]))
    before = prefix((retain_list[-1], local_mats[-1], local_vecs[-1]), "tm", chain_join, identity)
    pieces = [
        solve_rows(
            retain_list[p] * before[1] + local_mats[p],
            retain_list[p] * before[2] + local_vecs[p],
            row_start,
            row_share,
        )
        for p in range(segments_here)
    ]
    factor = jnp.stack([piece[0] for piece in pieces], axis=0)
    state = jnp.stack([piece[1] for piece in pieces], axis=0)
    return (factor, state)


def solution(mesh):
    in_specs = (P("tm", "rows", None), P("tm", "rows"), P("tm"), P("tm"))
    out_specs = (P("tm", "rows", None), P("tm", "rows"))
    return jax.shard_map(
        on_device, mesh=mesh, in_specs=in_specs, out_specs=out_specs, check_vma=False
    )
```

profile of v0, /device:TPU:0, one launch (start us, length us, event | category | flops | bytes accessed | tf_op | source)
XLA Modules:
  0.0 470.8 jit_solution(10219128800556037700)
XLA Ops:
  8.3 2.1 fusion.117
  11.8 104.5 %all-reduce.4.cloned.1.call-done = f32[2,512,512]{1,2,0:T(8,128)} async-done(((f32[2,512,512]{1,2,0:T(8,128)}), f32[2,512,512]{1,2,0:T(8,128)}) %all-reduce.4.cloned.1.call-update) | async-done | bytes 2097168 | tf_op jit(solution)/shard_map/psum | solution.py:63
  116.2 2.5 multiply_add_fusion
  118.7 1.3 copy.22
  122.7 6.3 %all-reduce.1 = f32[4]{0:T(128)S(1)} all-reduce(f32[4]{0:T(128)S(1)} %dynamic-update-slice.20), channel_id=1, replica_groups=mesh['rows'=8,'tm'=4] {'tm'}, use_global_device_ids=true, to_apply=%add.1 | all-reduce | flops 4 | bytes 32
  129.2 20.6 %psum.15 = f32[2,512]{1,0:T(2,128)S(1)} all-reduce(f32[2,512]{1,0:T(2,128)S(1)} %bitcast.351), channel_id=1, replica_groups=mesh['rows'=8,'tm'=4] {'rows'}, use_global_device_ids=true, to_apply=%region_1.0 | all-reduce | flops 1024 | bytes 8192 | tf_op jit(solution)/shard_map/psum | solution.py:63
  150.5 5.2 %all-gather = f32[4,1,512]{2,1,0:T(1,128)S(1)} all-gather(f32[1,1,512]{2,1,0:T(1,128)S(1)} %get-tuple-element.233), channel_id=1, replica_groups=mesh['rows'=8,'tm'=4] {'tm'}, dimensions={0}, use_global_device_ids=true | all-gather | bytes 10240 | tf_op jit(solution)/shard_map/all_gather | solution.py:9
  155.7 10.8 %while.24 = (s32[]{:T(128)}, f32[512,512]{1,0:T(8,128)S(1)}, f32[512]{0:T(512)S(1)}, s32[]{:T(128)}, f32[4]{0:T(128)S(1)}, /*index=5*/f32[4,512,512]{2,1,0:T(8,128)}, f32[4,512]{1,0:T(4,128)S(1)}, s32[]{:T(128)}, s32[]{:T(128)}) while((s32[]{:T(128)}, f32[512,512]{1,0:T(8,128)S(1)}, f32[512]{0:T(512)S(1)}, s32[]{:T(128)}, ...), condition=%wide.region_3.4_spmd.clone, body=%wide.region_2.3_spmd.clone.sunk | while | flops 1050628 | bytes 3156111 | solution.py:18
  156.2 2.3 fusion.142
  159.8 2.3 fusion.142
  163.3 2.3 fusion.142
  166.5 1.3 copy.23
  167.8 3.5 bitcast_add_fusion.4
  171.3 1.3 copy.24
  172.6 1.4 copy.29
  174.0 3.1 fusion.25
  178.1 11.7 %cholesky.286 = f32[128,128]{1,0:T(8,128)S(1)} custom-call(f32[128,128]{1,0:T(8,128)S(1)} %cholesky.426), custom_call_target="Cholesky" | custom-call | tf_op jit(solution)/shard_map/jit(cholesky)/cholesky | solution.py:45
  189.8 9.8 %custom-call.33 = f32[1,128,128]{1,2,0:T(8,128)S(1)} custom-call(f32[1,128,128]{2,1,0:T(8,128)S(1)} %get-tuple-element.250), custom_call_target="InvertDiagBlocksLowerTriangular" | custom-call | tf_op jit(solution)/shard_map/jit(cholesky)/cholesky | solution.py:45
  199.7 1.3 fusion.40
  201.1 1.4 convolution_subtract_fusion.1
  203.4 12.1 %cholesky.358 = f32[128,128]{1,0:T(8,128)S(1)} custom-call(f32[128,128]{1,0:T(8,128)S(1)} %cholesky.439), custom_call_target="Cholesky" | custom-call | tf_op jit(solution)/shard_map/jit(cholesky)/cholesky | solution.py:45
  215.5 9.8 %custom-call.36 = f32[1,128,128]{1,2,0:T(8,128)S(1)} custom-call(f32[1,128,128]{2,1,0:T(8,128)S(1)} %get-tuple-element.260), custom_call_target="InvertDiagBlocksLowerTriangular" | custom-call | tf_op jit(solution)/shard_map/jit(cholesky)/cholesky | solution.py:45
  225.3 1.3 fusion.37
  226.8 1.4 convolution_subtract_fusion
  228.4 11.7 %cholesky.305 = f32[128,128]{1,0:T(8,128)S(1)} custom-call(f32[128,128]{1,0:T(8,128)S(1)} %cholesky.430), custom_call_target="Cholesky" | custom-call | tf_op jit(solution)/shard_map/jit(cholesky)/cholesky | solution.py:45
  241.4 9.8 %custom-call.34 = f32[1,128,128]{1,2,0:T(8,128)S(1)} custom-call(f32[1,128,128]{2,1,0:T(8,128)S(1)} %get-tuple-element.247), custom_call_target="InvertDiagBlocksLowerTriangular" | custom-call | tf_op jit(solution)/shard_map/jit(cholesky)/cholesky | solution.py:45
  251.5 1.3 convolution_subtract_fusion.3
  252.8 11.9 %cholesky.326 = f32[128,128]{1,0:T(8,128)S(1)} custom-call(f32[128,128]{1,0:T(8,128)S(1)} %cholesky.435), custom_call_target="Cholesky" | custom-call | tf_op jit(solution)/shard_map/jit(cholesky)/cholesky | solution.py:45
  265.4 9.8 %custom-call.35 = f32[1,128,128]{1,2,0:T(8,128)S(1)} custom-call(f32[1,128,128]{2,1,0:T(8,128)S(1)} %get-tuple-element.244), custom_call_target="InvertDiagBlocksLowerTriangular" | custom-call | tf_op jit(solution)/shard_map/jit(cholesky)/cholesky | solution.py:45
  276.7 11.7 %cholesky.343 = f32[128,128]{1,0:T(8,128)S(1)} custom-call(f32[128,128]{1,0:T(8,128)S(1)} %convolution_subtract_fusion.5), custom_call_target="Cholesky" | custom-call | tf_op jit(solution)/shard_map/jit(cholesky)/cholesky | solution.py:45
  293.0 7.9 %while.25 = (s32[]{:T(128)}, f32[512,512]{1,0:T(8,128)S(1)}, s32[4,2]{0,1:T(2,128)S(1)}, f32[4,128,128]{2,1,0:T(8,128)S(1)}, s32[]{:T(128)}) while((s32[]{:T(128)}, f32[512,512]{1,0:T(8,128)S(1)}, s32[4,2]{0,1:T(2,128)S(1)}, f32[4,128,128]{2,1,0:T(8,128)S(1)}, s32[]{:T(128)}) %tuple.104), condition=%wide.while_cond.1, body=%wide.while_body.1.sunk | while | flops 2 | bytes 131181 | solution.py:47
  293.6 1.4 bitcast_dynamic-update-slice_fusion.4
  295.6 1.4 bitcast_dynamic-update-slice_fusion.4
  297.5 1.4 bitcast_dynamic-update-slice_fusion.4
  299.5 1.4 bitcast_dynamic-update-slice_fusion.4
  300.9 39.5 %custom-call.40 = f32[4,128,128]{1,2,0:T(8,128)S(1)} custom-call(f32[4,128,128]{2,1,0:T(8,128)S(1)} %get-tuple-element.185), custom_call_target="InvertDiagBlocksLowerTriangular" | custom-call | tf_op jit(solution)/shard_map/jit(_solve_triangular)/triangular_solve | solution.py:47
  344.8 11.7 %cholesky.377 = f32[128,128]{1,0:T(8,128)S(1)} custom-call(f32[128,128]{1,0:T(8,128)S(1)} %cholesky.443), custom_call_target="Cholesky" | custom-call | tf_op jit(solution)/shard_map/jit(cholesky)/cholesky | solution.py:45
  357.9 9.8 %custom-call.37 = f32[1,128,128]{1,2,0:T(8,128)S(1)} custom-call(f32[1,128,128]{2,1,0:T(8,128)S(1)} %get-tuple-element.257), custom_call_target="InvertDiagBlocksLowerTriangular" | custom-call | tf_op jit(solution)/shard_map/jit(cholesky)/cholesky | solution.py:45
  369.2 11.7 %cholesky.398 = f32[128,128]{1,0:T(8,128)S(1)} custom-call(f32[128,128]{1,0:T(8,128)S(1)} %cholesky.448), custom_call_target="Cholesky" | custom-call | tf_op jit(solution)/shard_map/jit(cholesky)/cholesky | solution.py:45
  381.7 10.0 %custom-call.38 = f32[1,128,128]{1,2,0:T(8,128)S(1)} custom-call(f32[1,128,128]{2,1,0:T(8,128)S(1)} %get-tuple-element.254), custom_call_target="InvertDiagBlocksLowerTriangular" | custom-call | tf_op jit(solution)/shard_map/jit(cholesky)/cholesky | solution.py:45
  393.1 11.7 %cholesky.415 = f32[128,128]{1,0:T(8,128)S(1)} custom-call(f32[128,128]{1,0:T(8,128)S(1)} %convolution_subtract_fusion.4), custom_call_target="Cholesky" | custom-call | tf_op jit(solution)/shard_map/jit(cholesky)/cholesky | solution.py:45
  408.2 1.3 fusion.28
  409.5 7.9 %while.26 = (s32[]{:T(128)}, f32[512,512]{1,0:T(8,128)S(1)}, s32[4,2]{0,1:T(2,128)S(1)}, f32[4,128,128]{2,1,0:T(8,128)S(1)}, s32[]{:T(128)}) while((s32[]{:T(128)}, f32[512,512]{1,0:T(8,128)S(1)}, s32[4,2]{0,1:T(2,128)S(1)}, f32[4,128,128]{2,1,0:T(8,128)S(1)}, s32[]{:T(128)}) %tuple.111), condition=%wide.while_cond.1.clone, body=%wide.while_body.1.clone.sunk | while | flops 2 | bytes 131181 | solution.py:47
  410.1 1.4 bitcast_dynamic-update-slice_fusion.5
  412.1 1.4 bitcast_dynamic-update-slice_fusion.5
  414.1 1.4 bitcast_dynamic-update-slice_fusion.5
  416.0 1.4 bitcast_dynamic-update-slice_fusion.5
  417.4 39.3 %custom-call.42 = f32[4,128,128]{1,2,0:T(8,128)S(1)} custom-call(f32[4,128,128]{2,1,0:T(8,128)S(1)} %get-tuple-element.187), custom_call_target="InvertDiagBlocksLowerTriangular" | custom-call | tf_op jit(solution)/shard_map/jit(_solve_triangular)/triangular_solve | solution.py:47
  (133 shorter events, 37.4 us)
Async XLA Ops:
  7.2 1.1 copy-start
  7.2 3.3 copy-start.3
  7.2 3.3 copy-start.4
  7.2 109.0 %all-reduce.4.cloned.1.call-start = ((), (), s32[]{:S(2)}) async-start(), calls=%async_computation | async-start | bytes 4194304 | tf_op jit(solution)/shard_map/psum | solution.py:63
  10.4 145.2 %all-gather.3.cloned.1.call-start = ((), (), s32[]{:S(2)}) async-start(), calls=%async_computation.1 | async-start | bytes 5242880 | tf_op jit(solution)/shard_map/all_gather | solution.py:9
  118.7 2.7 copy-start.5
  118.7 10.3 %copy-start.2 = (bf16[2,384]{1,0:T(2,128)(2,1)S(1)}, bf16[2,384]{1,0:T(2,128)(2,1)}, u32[]{:S(2)}) copy-start(bf16[2,384]{1,0:T(2,128)(2,1)} %param.12) | copy-start | bytes 4612
  177.1 1.0 copy-start.1
Sparse Core Ops, SparseCore 0:
  11.7 104.5 all-reduce.3
  120.2 34.2 all-gather.2
where the time goes:
time: 475 us; the launch traced here: 471 us
  other arithmetic  261 us (55%)
  waiting for transfers between devices  104 us (22%)
  blocking collectives  32 us (7%)
  local copies, waits for them, and re-layouts  31.6 us (7%)
  between operations  21.9 us (5%)
  matrix products  19.6 us (4%)
    another operation x30, other arithmetic, solve_rows(): lower_factor = jnp.linalg.cholesky(matrix)  159 us
    psum x1, waiting for transfers between devices, on_device(): information, projected = lax.psum((partial_value, gradient), 'rows')  104 us
    another operation x7, other arithmetic, solve_rows(): jax.scipy.linalg.solve_triangular(lower_factor, middle, lower=True, trans=1)  81.4 us
    psum x1, blocking collectives, on_device(): information, projected = lax.psum((partial_value, gradient), 'rows')  20.6 us
    another operation x27, local copies, waits for them, and re-layouts, solve_rows(): jax.scipy.linalg.solve_triangular(lower_factor, middle, lower=True, trans=1)  15.7 us
    another operation x12, matrix products, solve_rows(): lower_factor = jnp.linalg.cholesky(matrix)  11.4 us
  transfers between devices with their start and end apart: 2, of which 1 were waited for; matrix products, arithmetic and copies ran while one was open for 1% of the time, Pallas kernels for 0%

commit v1 on v0

v1 whole, which is shorter than its diff:
```python
import functools

import jax
import jax.numpy as jnp
from jax import lax
from jax.experimental import pallas as pl
from jax.experimental.pallas import tpu as pltpu
from jax.sharding import PartitionSpec as P

HIGHEST = lax.Precision.HIGHEST
LANES = 128
GROUP = 8


def dot(a, b, over_a, over_b):
    return lax.dot_general(
        a, b, (((over_a,), (over_b,)), ((), ())),
        precision=HIGHEST, preferred_element_type=jnp.float32,
    )


def lane_spread(tile, lane):
    return jnp.broadcast_to(tile[:, lane : lane + 1], tile.shape)


def row_spread(tile, row):
    return jnp.broadcast_to(tile[row : row + 1, :], tile.shape)


def factor_tiles(many):
    lane = lax.broadcasted_iota(jnp.int32, (GROUP, LANES), 1)
    sub = lax.broadcasted_iota(jnp.int32, (GROUP, LANES), 0)
    many = [list(tiles) for tiles in many]
    count = len(many[0])
    here = range(len(many))
    over = [jnp.ones((GROUP, LANES), jnp.float32) for _ in here]
    pivots = [[None] * count for _ in here]
    for g in range(count):
        top = [many[s][g] for s in here]
        cols = [[lane_spread(top[s], g * GROUP + k) for k in range(GROUP)] for s in here]
        inverse = [[None] * GROUP for _ in here]
        rows = [[None] * GROUP for _ in here]
        heads = [[None] * GROUP for _ in here]
        for k in range(GROUP):
            at = g * GROUP + k
            for s in here:
                head = [None] * (k + 1) + [row_spread(c, k) for c in cols[s][k + 1 :]]
                pivot = row_spread(cols[s][k], k)
                inv = 1.0 / pivot
                times = jnp.where(sub > k, cols[s][k] * inv, 0.0)
                row = row_spread(top[s], k)
                row = jnp.where(lane == at, row + row, row)
                top[s] = top[s] - times * row
                for later in range(k + 1, GROUP):
                    cols[s][later] = cols[s][later] - times * head[later]
                inverse[s][k], rows[s][k], heads[s][k] = inv, row, head
                over[s] = jnp.where(lane == at, inv, over[s])
                pivots[s][g] = pivot if k == 0 else jnp.where(sub >= k, pivot, pivots[s][g])
        for s in here:
            many[s][g] = top[s]
        for v in range(g + 1, count):
            for s in here:
                tile = many[s][v]
                mine = [lane_spread(tile, g * GROUP + k) for k in range(GROUP)]
                for k in range(GROUP):
                    times = mine[k] * inverse[s][k]
                    tile = tile - times * rows[s][k]
                    for later in range(k + 1, GROUP):
                        mine[later] = mine[later] - times * heads[s][k][later]
                many[s][v] = tile
    upper, lower = [], []
    for s in here:
        ups, lows = [], []
        for g in range(count):
            scale = lax.rsqrt(pivots[s][g])
            tile = many[s][g] * scale
            at = sub + g * GROUP
            ups.append(jnp.where(lane >= at, tile, 0.0))
            lows.append(jnp.where(lane <= at, tile * over[s], 0.0))
        upper.append(ups)
        lower.append(lows)
    return upper, lower


def smoother_kernel(start_ref, mats_ref, vecs_ref, rows_ref, state_ref, work, inv, vec):
    segs, width = mats_ref.shape[0], mats_ref.shape[1]
    blocks = width // LANES
    tiles = LANES // GROUP
    for s in range(segs):
        work[s] = mats_ref[s]
        vec[s] = jnp.broadcast_to(vecs_ref[s], (GROUP, width))

    def block_step(b, carry):
        base = pl.multiple_of(b * LANES, LANES)
        square = [
            [work[s, pl.ds(pl.multiple_of(base + t * GROUP, GROUP), GROUP), pl.ds(base, LANES)] for t in range(tiles)]
            for s in range(segs)
        ]
        upper, lower = factor_tiles(square)
        for s in range(segs):
            for t in range(tiles):
                work[s, pl.ds(pl.multiple_of(base + t * GROUP, GROUP), GROUP), pl.ds(base, LANES)] = upper[s][t]
                inv[s, pl.ds(pl.multiple_of(base + t * GROUP, GROUP), GROUP), :] = lower[s][t]

        for i in range(blocks):
            @pl.when(b == i)
            def _(i=i):
                lo, hi = i * LANES, (i + 1) * LANES
                for s in range(segs):
                    low = inv[s, lo:hi, :]
                    y = dot(vec[s, :, lo:hi], low, 1, 1)
                    vec[s, :, lo:hi] = y
                    if i < blocks - 1:
                        panel = dot(low, work[s, lo:hi, hi:], 1, 0)
                        work[s, lo:hi, hi:] = panel
                        vec[s, :, hi:] = vec[s, :, hi:] - dot(y, panel, 1, 0)
                        for j in range(i + 1, blocks):
                            left = (j - i - 1) * LANES
                            jl, jh = j * LANES, (j + 1) * LANES
                            work[s, jl:jh, jl:] = work[s, jl:jh, jl:] - dot(
                                panel[:, left : left + LANES], panel[:, left:], 0, 0
                            )
                            work[s, jl:jh, lo:hi] = jnp.zeros((LANES, LANES), jnp.float32)
        return carry

    lax.fori_loop(0, blocks, block_step, 0)
    for b in reversed(range(blocks)):
        lo, hi = b * LANES, (b + 1) * LANES
        for s in range(segs):
            right = vec[s, :, lo:hi]
            if b < blocks - 1:
                right = right - dot(vec[s, :, hi:], work[s, lo:hi, hi:], 1, 1)
            vec[s, :, lo:hi] = dot(right, inv[s, lo:hi, :], 1, 0)
    share = rows_ref.shape[1]
    start = pl.multiple_of(start_ref[0], GROUP)
    for s in range(segs):
        rows_ref[s] = work[s, pl.ds(start, share), :]
        state_ref[s] = vec[s]


def smooth(mats, vecs, row_start, row_share):
    segs, width = mats.shape[0], mats.shape[1]
    vmem = pl.BlockSpec(memory_space=pltpu.VMEM)
    rows, state = pl.pallas_call(
        smoother_kernel,
        out_shape=(
            jax.ShapeDtypeStruct((segs, row_share, width), jnp.float32),
            jax.ShapeDtypeStruct((segs, GROUP, width), jnp.float32),
        ),
        in_specs=[pl.BlockSpec(memory_space=pltpu.SMEM), vmem, vmem],
        out_specs=(vmem, vmem),
        scratch_shapes=[
            pltpu.VMEM((segs, width, width), jnp.float32),
            pltpu.VMEM((segs, width, LANES), jnp.float32),
            pltpu.VMEM((segs, GROUP, width), jnp.float32),
        ],
        compiler_params=pltpu.CompilerParams(vmem_limit_bytes=40 * 1024 * 1024),
        cost_estimate=pl.CostEstimate(
            flops=2 * segs * width**3, bytes_accessed=8 * segs * width**2, transcendentals=0
        ),
    )(jnp.reshape(row_start, (1,)), mats, vecs.reshape(segs, 1, width))
    return rows, lax.dynamic_slice_in_dim(state[:, 0, :], row_start, row_share, 1)


def on_device(jacobian, rhs, forget, restart):
    segments_here, _, state_width = jacobian.shape
    row_share = state_width // lax.axis_size("rows")
    row_start = lax.axis_index("rows") * row_share
    decays = forget * (1.0 - 0.2 * restart.astype(jnp.float32))
    partial_value = jnp.einsum(
        "srv,srw->svw", jacobian, jacobian, preferred_element_type=jnp.float32
    )
    gradient = jnp.einsum("sr,srv->sv", rhs, jacobian, preferred_element_type=jnp.float32)
    both = jnp.concatenate([partial_value, gradient[:, None, :]], axis=1)
    both = lax.psum(both, "rows")
    local, retained = [both[0]], [decays[0]]
    for s in range(1, segments_here):
        local.append(decays[s] * local[-1] + both[s])
        retained.append(decays[s] * retained[-1])
    count, mine = lax.axis_size("tm"), lax.axis_index("tm")
    ends = lax.all_gather(local[-1], "tm")
    keeps = lax.all_gather(retained[-1], "tm")
    before = jnp.zeros_like(local[0])
    for t in range(count - 1):
        before = jnp.where(t < mine, keeps[t] * before + ends[t], before)
    post = jnp.stack([retained[s] * before + local[s] for s in range(segments_here)])
    return smooth(post[:, :state_width], post[:, state_width], row_start, row_share)


def solution(mesh):
    in_specs = (P("tm", "rows", None), P("tm", "rows"), P("tm"), P("tm"))
    out_specs = (P("tm", "rows", None), P("tm", "rows"))
    return jax.shard_map(
        on_device, mesh=mesh, in_specs=in_specs, out_specs=out_specs, check_vma=False
    )
```

time: 475 us -> 198 us (0.42)
  other arithmetic: 261 us -> 10.6 us
  Pallas kernels: 0 us -> 28.9 us
  local copies, waits for them, and re-layouts: 31.6 us -> 4.94 us
  waiting for transfers between devices: 104 us -> 130 us
  blocking collectives: 32 us -> 6.28 us
  matrix products: 19.6 us -> 0.95 us
  between operations: 21.9 us -> 16.1 us
    another operation x41 -> x2, other arithmetic: 241 us -> 0.18 us  [on_device(): jnp.stack([retained[s] * before + local[s] for s in range(segments_here)])]
    pallas_call x0 -> x1, Pallas kernels: none -> 28.9 us  [smooth(): pl.pallas_call(smoother_kernel, out_shape=(jax.ShapeDtypeStruct((segs, ro...]
    all_gather x1, waiting for transfers between devices: 0.01 us -> 24.5 us  [on_device(): ends = lax.all_gather(local[-1], 'tm')]
    psum x1 -> x0, blocking collectives: 20.6 us -> none  [on_device(): information, projected = lax.psum((partial_value, gradient), 'rows')]
    another operation x43 -> x0, local copies, waits for them, and re-layouts: 19.4 us -> none  [the longest x27 15.7 us: solve_rows(): jax.scipy.linalg.solve_triangular(lower_factor, middle, lower=True, trans=1)]
    another operation x40 -> x0, matrix products: 17.2 us -> none  [the longest x12 11.4 us: solve_rows(): lower_factor = jnp.linalg.cholesky(matrix)]
    select_n x6 -> x0, other arithmetic: 8.74 us -> none  [turn(): jnp.where(position < mine, new, old)]
    all_gather x1 -> x0, blocking collectives: 5.17 us -> none  [prefix(): pieces = jax.tree.map(lambda part: lax.all_gather(part, axis), value)]
  transfers between devices with their start and end apart: 2 -> 2, of which waited for: 1 -> 2; matrix products, arithmetic and copies ran while one was open for 1% -> 1% of each run, Pallas kernels for 0% -> 0%
where the time goes in v1:
time: 198 us; the launch traced here: 197 us
  waiting for transfers between devices  130 us (66%)
  Pallas kernels  28.9 us (15%)
  between operations  16.1 us (8%)
  other arithmetic  10.6 us (5%)
  blocking collectives  6.28 us (3%)
  local copies, waits for them, and re-layouts  4.94 us (2%)
    psum x1, waiting for transfers between devices, on_device(): both = lax.psum(both, 'rows')  105 us
    pallas_call x1, Pallas kernels, smooth(): pl.pallas_call(smoother_kernel, out_shape=(jax.ShapeDtypeStruct((segs, ro...  28.9 us
    all_gather x1, waiting for transfers between devices, on_device(): ends = lax.all_gather(local[-1], 'tm')  24.5 us
    unnamed x1, blocking collectives  6.28 us
    add x2, other arithmetic, on_device(): retained[s] * before + local[s]  5.31 us
  transfers between devices with their start and end apart: 2, of which 2 were waited for; matrix products, arithmetic and copies ran while one was open for 1% of the time, Pallas kernels for 0%

profile of v1, /device:TPU:0, one launch (start us, length us, event | category | flops | bytes accessed | tf_op | source)
XLA Modules:
  0.0 197.4 jit_solution(6649609312697638295)
XLA Ops:
  7.2 0.0 copy-start
  7.2 0.0 copy-start.2
  7.2 0.0 all-reduce.3.cloned.1.call-start
  7.2 1.1 copy-done
  8.3 0.7 fusion.9
  9.1 0.0 copy-done.2
  9.1 0.2 fusion.4
  9.3 1.5 pad_maximum_fusion
  10.8 0.0 copy-start.3
  10.8 0.0 copy-start.4
  10.8 0.0 all-reduce.3.cloned.1.call-update
  10.8 0.0 all-gather.2.cloned.1.call-start
  10.9 0.6 copy-done.3
  11.5 0.0 copy-done.4
  11.5 0.6 fusion.8
  12.1 105.0 %all-reduce.3.cloned.1.call-done = f32[2,513,512]{2,1,0:T(8,128)} async-done(((f32[2,513,512]{2,1,0:T(8,128)}), f32[2,513,512]{2,1,0:T(8,128)}) %all-reduce.3.cloned.1.call-update) | async-done | bytes 2101264 | tf_op jit(solution)/shard_map/psum | solution.py:175
  117.1 0.0 copy-start.1
  117.1 3.6 %slice_add_fusion.3 = f32[1,513,512]{2,1,0:T(8,128)} fusion(f32[2,513,512]{2,1,0:T(8,128)} %all-reduce.3.cloned.1.call-done, f32[]{:T(128)} %bitcast.2), kind=kLoop, calls=%fused_computation.10 | loop fusion | flops 525312 | bytes 3151876 | tf_op jit(solution)/shard_map/add | solution.py:178
  120.7 0.0 copy-start.5
  120.7 0.0 all-gather.2.cloned.1.call-update
  122.0 0.0 copy-done.5
  122.0 0.6 dynamic-slice.1
  122.6 0.8 dynamic-update-slice
  123.3 6.3 %all-reduce = f32[4]{0:T(128)S(1)} all-reduce(f32[4]{0:T(128)S(1)} %dynamic-update-slice), channel_id=1, replica_groups=mesh['rows'=8,'tm'=4] {'tm'}, use_global_device_ids=true, to_apply=%add | all-reduce | flops 4 | bytes 32
  129.6 0.7 fusion.7
  131.0 24.5 %all-gather.2.cloned.1.call-done = f32[4,513,512]{2,1,0:T(8,128)} async-done(((f32[1,513,512]{2,1,0:T(8,128)}), f32[4,513,512]{2,1,0:T(8,128)}) %all-gather.2.cloned.1.call-update) | async-done | bytes 4202512 | tf_op jit(solution)/shard_map/all_gather | solution.py:181
  155.5 0.0 copy-done.1
  155.5 4.4 %multiply_add_fusion = (f32[1,513,512]{2,1,0:T(8,128)S(1)}, f32[1,513,512]{2,1,0:T(8,128)S(1)}) fusion(f32[]{:T(128)} %mul.64, f32[4,513,512]{2,1,0:T(8,128)} %all-gather.2.cloned.1.call-done, f32[]{:T(128)} %bitcast.7, pred[]{:T(512)S(6)} %gt.11, f32[]{:T(128)} %bitcast.6, pred[]{:T(512)S(6)} %gt.10, f32[]{:T(128)} %bitcast.5, pred[]{:T(512)S(6)} %gt.9, ...), kind=kLoop, calls=%fused_computation.11 | loop fusion | flops 3151872 | bytes 7354391 | tf_op jit(solution)/shard_map/add | solution.py:186
  159.9 0.9 multiply_add_fusion.1
  160.8 0.2 fusion.mats_ref
  161.0 28.9 %shard_map.59 = (f32[2,64,512]{2,1,0:T(8,128)}, f32[2,8,512]{2,1,0:T(8,128)S(1)}) custom-call(s32[1]{0:T(128)} %bitcast.start_ref, f32[2,512,512]{2,1,0:T(8,128)S(1)} %fusion.mats_ref, f32[2,1,512]{2,1,0:T(1,128)S(1)} %pad_maximum_fusion.1.vecs_ref), custom_call_target="tpu_custom_call" | custom-call | flops 536870912 | bytes 4194304 | tf_op jit(solution)/shard_map/pallas_call | solution.py:144
  189.9 0.6 constant_dynamic-slice_fusion
  (6 shorter events, 0.0 us)
Async XLA Ops:
  7.2 1.1 copy-start
  7.2 1.9 copy-start.2
  7.2 109.9 %all-reduce.3.cloned.1.call-start = ((), (), s32[]{:S(2)}) async-start(), calls=%async_computation | async-start | bytes 4259840 | tf_op jit(solution)/shard_map/psum | solution.py:175
  10.8 0.7 copy-start.3
  10.8 0.7 copy-start.4
  10.8 144.6 %all-gather.2.cloned.1.call-start = ((), (), s32[]{:S(2)}) async-start(), calls=%async_computation.1 | async-start | bytes 5324800 | tf_op jit(solution)/shard_map/all_gather | solution.py:181
  117.1 38.4 %copy-start.1 = (f32[2,513,512]{2,1,0:T(8,128)S(1)}, f32[2,513,512]{2,1,0:T(8,128)}, u32[]{:S(2)}) copy-start(f32[2,513,512]{2,1,0:T(8,128)} %all-reduce.3.cloned.1.call-done) | copy-start | bytes 6303748
  120.7 1.3 copy-start.5
Sparse Core Ops, SparseCore 0:
  11.6 105.4 all-reduce.2
  120.8 34.5 all-gather.1

commit v2 on v1

--- a/solution.py
+++ b/solution.py
@@ -82,13 +82,199 @@
     return upper, lower
 
 
-def smoother_kernel(start_ref, mats_ref, vecs_ref, rows_ref, state_ref, work, inv, vec):
-    segs, width = mats_ref.shape[0], mats_ref.shape[1]
+def tile_list(width):
+    blocks = width // LANES
+    return [(i, j) for i in range(blocks) for j in range(i, blocks)]
+
+
+def shard_rows(width, count):
+    rows = len(tile_list(width)) * LANES + GROUP
+    return -(-rows // (count * GROUP)) * GROUP
+
+
+def gram_kernel(decay_ref, jac_ref, rhs_ref, out_ref):
+    count, _, share, _ = out_ref.shape
+    width = jac_ref.shape[2]
+    tiles = tile_list(width)
+
+    def put(seg, row, value):
+        done = 0
+        while done < value.shape[0]:
+            owner, at = divmod(row + done, share)
+            step = min(share - at, value.shape[0] - done)
+            out_ref[owner, seg, at : at + step, :] = value[done : done + step, :]
+            done += step
+
+    keep = decay_ref[1]
+    for i in range(width // LANES):
+        lo, hi = i * LANES, (i + 1) * LANES
+        first, second = [
+            lax.dot_general(
+                jac_ref[s, :, lo:hi], jac_ref[s, :, lo:], (((0,), (0,)), ((), ())),
+                preferred_element_type=jnp.float32,
+            )
+            for s in range(2)
+        ]
+        second = keep * first + second
+        for j in range(i, width // LANES):
+            row = tiles.index((i, j)) * LANES
+            left = (j - i) * LANES
+            put(0, row, first[:, left : left + LANES])
+            put(1, row, second[:, left : left + LANES])
+    row = len(tiles) * LANES
+    vecs = [
+        jnp.dot(rhs_ref[s : s + 1, :], jac_ref[s], preferred_element_type=jnp.float32) for s in range(2)
+    ]
+    vecs[1] = keep * vecs[0] + vecs[1]
+    for s in range(2):
+        parts = [vecs[s][:, lo : lo + LANES] for lo in range(0, width, LANES)]
+        pad = jnp.zeros((count * share - row - len(parts), LANES), jnp.float32)
+        put(s, row, jnp.concatenate(parts + [pad], axis=0))
+
+
+def gram(decays, jacobian, rhs, count):
+    width = jacobian.shape[2]
+    vmem = pl.BlockSpec(memory_space=pltpu.VMEM)
+    return pl.pallas_call(
+        gram_kernel,
+        out_shape=jax.ShapeDtypeStruct((count, 2, shard_rows(width, count), LANES), jnp.float32),
+        in_specs=[pl.BlockSpec(memory_space=pltpu.SMEM), vmem, vmem],
+        out_specs=vmem,
+        compiler_params=pltpu.CompilerParams(vmem_limit_bytes=40 * 1024 * 1024),
+    )(decays, jacobian, rhs)
+
+
+def exchange_kernel(
+    count, steps, decay_ref, part_ref, out_ref, near, far, mine, past, post, prior, weight,
+    near_send, near_recv, far_send, far_recv, past_send, past_recv, post_send, post_recv,
+):
+    me, now = lax.axis_index("rows"), lax.axis_index("tm")
+    half, share = count // 2, out_ref.shape[1]
+    line, side = me // 2, me % 2
+
+    barrier = pltpu.get_barrier_semaphore()
+    for j in range(1, count):
+        pl.semaphore_signal(
+            barrier, inc=1, device_id=((me + j) % count, now), device_id_type=pl.DeviceIdType.MESH
+        )
+    for j in range(1, steps):
+        pl.semaphore_signal(
+            barrier, inc=1, device_id=(me, (now + j) % steps), device_id_type=pl.DeviceIdType.MESH
+        )
+    pl.semaphore_wait(barrier, count + steps - 2)
+
+    def send(src, dst, send_sem, recv_sem, row, step):
+        return pltpu.make_async_remote_copy(
+            src_ref=src, dst_ref=dst, send_sem=send_sem, recv_sem=recv_sem,
+            device_id=(row, step), device_id_type=pl.DeviceIdType.MESH,
+        )
+
+    order = list(range(1, half)) + [0]
+    first = {}
+    for j in order:
+        owner = 2 * ((line + j) % half) + (1 - side)
+        first[j] = send(
+            part_ref.at[owner], near.at[j], near_send.at[j], near_recv.at[j], 2 * line + (1 - side), now
+        )
+        first[j].start()
+    second = {}
+    for j in order:
+        first[j].wait_recv()
+        owner = 2 * ((line + j) % half) + side
+        near[j] = near[j] + part_ref[owner]
+        if j:
+            second[j] = send(near.at[j], far.at[j], far_send.at[j], far_recv.at[j], owner, now)
+            second[j].start()
+    total = near[0]
+    for j in range(1, half):
+        second[j].wait_recv()
+        total = total + far[j]
+    keep0, keep1 = decay_ref[0], decay_ref[1]
+    mine[:, :share, :] = total
+    mine[:, share:, :] = jnp.full((2, GROUP, LANES), keep0 * keep1, jnp.float32)
+
+    passed = {}
+    for j in range(1, steps):
+        passed[j] = send(
+            mine.at[1], past.at[j], past_send.at[j], past_recv.at[j], me, (now + j) % steps
+        )
+
+        @pl.when(now + j < steps)
+        def _(j=j):
+            passed[j].start()
+
+    prior[...] = jnp.zeros_like(prior)
+    weight[...] = jnp.ones_like(weight)
+    for j in range(1, steps):
+        @pl.when(now >= j)
+        def _(j=j):
+            passed[j].wait_recv()
+            prior[...] = prior[...] + weight[0:1, :] * past[j, :share, :]
+            weight[...] = weight[...] * past[j, share:, :]
+
+    post[0] = keep0 * prior[...] + mine[0, :share, :]
+    post[1] = (keep0 * keep1) * prior[...] + mine[1, :share, :]
+
+    last = {}
+    for j in range(1, count):
+        other = (me + j) % count
+        last[j] = send(
+            post.at[other % 2], out_ref.at[me], post_send.at[j], post_recv.at[j], other, now
+        )
+        last[j].start()
+    out_ref[me] = post[side]
+    for j in range(1, count):
+        last[j].wait_recv()
+    for j in order:
+        first[j].wait_send()
+        if j:
+            second[j].wait_send()
+    for j in range(1, steps):
+        @pl.when(now + j < steps)
+        def _(j=j):
+            passed[j].wait_send()
+    for j in range(1, count):
+        last[j].wait_send()
+
+
+def exchange(decays, parts, count, steps):
+    share = parts.shape[2]
+    half = count // 2
+    vmem = pl.BlockSpec(memory_space=pltpu.VMEM)
+    dma = pltpu.SemaphoreType.DMA
+    f32 = jnp.float32
+    return pl.pallas_call(
+        functools.partial(exchange_kernel, count, steps),
+        out_shape=jax.ShapeDtypeStruct((count, share, LANES), f32),
+        in_specs=[pl.BlockSpec(memory_space=pltpu.SMEM), vmem],
+        out_specs=vmem,
+        scratch_shapes=[
+            pltpu.VMEM((half, 2, share, LANES), f32),
+            pltpu.VMEM((half, 2, share, LANES), f32),
+            pltpu.VMEM((2, share + GROUP, LANES), f32),
+            pltpu.VMEM((steps, share + GROUP, LANES), f32),
+            pltpu.VMEM((2, share, LANES), f32),
+            pltpu.VMEM((share, LANES), f32),
+            pltpu.VMEM((GROUP, LANES), f32),
+            dma((half,)), dma((half,)), dma((half,)), dma((half,)),
+            dma((steps,)), dma((steps,)), dma((count,)), dma((count,)),
+        ],
+        compiler_params=pltpu.CompilerParams(
+            collective_id=0, has_side_effects=True, vmem_limit_bytes=40 * 1024 * 1024
+        ),
+    )(decays, parts)
+
+
+def smoother_kernel(place_ref, flat_ref, rows_ref, work, inv, vec):
+    segs, width = work.shape[0], work.shape[1]
     blocks = width // LANES
     tiles = LANES // GROUP
-    for s in range(segs):
-        work[s] = mats_ref[s]
-        vec[s] = jnp.broadcast_to(vecs_ref[s], (GROUP, width))
+    packed = tile_list(width)
+    for q, (i, j) in enumerate(packed):
+        work[0, i * LANES : (i + 1) * LANES, j * LANES : (j + 1) * LANES] = flat_ref[q * LANES : (q + 1) * LANES, :]
+    for j in range(blocks):
+        row = len(packed) * LANES + j
+        vec[0, :, j * LANES : (j + 1) * LANES] = jnp.broadcast_to(flat_ref[row : row + 1, :], (GROUP, LANES))
 
     def block_step(b, carry):
         base = pl.multiple_of(b * LANES, LANES)
@@ -131,60 +317,48 @@
             if b < blocks - 1:
                 right = right - dot(vec[s, :, hi:], work[s, lo:hi, hi:], 1, 1)
             vec[s, :, lo:hi] = dot(right, inv[s, lo:hi, :], 1, 0)
-    share = rows_ref.shape[1]
-    start = pl.multiple_of(start_ref[0], GROUP)
-    for s in range(segs):
-        rows_ref[s] = work[s, pl.ds(start, share), :]
-        state_ref[s] = vec[s]
-
-
-def smooth(mats, vecs, row_start, row_share):
-    segs, width = mats.shape[0], mats.shape[1]
+    share = rows_ref.shape[1] - GROUP
+    for k in range(2):
+        start = pl.multiple_of(place_ref[k], GROUP)
+        rows_ref[k, :share, :] = work[0, pl.ds(start, share), :]
+        rows_ref[k, share:, :] = vec[0]
+
+
+def smooth(flat, width, row_start, other_start, row_share):
     vmem = pl.BlockSpec(memory_space=pltpu.VMEM)
-    rows, state = pl.pallas_call(
+    return pl.pallas_call(
         smoother_kernel,
-        out_shape=(
-            jax.ShapeDtypeStruct((segs, row_share, width), jnp.float32),
-            jax.ShapeDtypeStruct((segs, GROUP, width), jnp.float32),
-        ),
-        in_specs=[pl.BlockSpec(memory_space=pltpu.SMEM), vmem, vmem],
-        out_specs=(vmem, vmem),
+        out_shape=jax.ShapeDtypeStruct((2, row_share + GROUP, width), jnp.float32),
+        in_specs=[pl.BlockSpec(memory_space=pltpu.SMEM), vmem],
+        out_specs=vmem,
         scratch_shapes=[
-            pltpu.VMEM((segs, width, width), jnp.float32),
-            pltpu.VMEM((segs, width, LANES), jnp.float32),
-            pltpu.VMEM((segs, GROUP, width), jnp.float32),
+            pltpu.VMEM((1, width, width), jnp.float32),
+            pltpu.VMEM((1, width, LANES), jnp.float32),
+            pltpu.VMEM((1, GROUP, width), jnp.float32),
         ],
         compiler_params=pltpu.CompilerParams(vmem_limit_bytes=40 * 1024 * 1024),
         cost_estimate=pl.CostEstimate(
-            flops=2 * segs * width**3, bytes_accessed=8 * segs * width**2, transcendentals=0
+            flops=2 * width**3, bytes_accessed=8 * width**2, transcendentals=0
         ),
-    )(jnp.reshape(row_start, (1,)), mats, vecs.reshape(segs, 1, width))
-    return rows, lax.dynamic_slice_in_dim(state[:, 0, :], row_start, row_share, 1)
+    )(jnp.stack([row_start, other_start]), flat)
 
 
 def on_device(jacobian, rhs, forget, restart):
-    segments_here, _, state_width = jacobian.shape
-    row_share = state_width // lax.axis_size("rows")
-    row_start = lax.axis_index("rows") * row_share
+    width = jacobian.shape[2]
+    count, steps = lax.axis_size("rows"), lax.axis_size("tm")
+    row_share = width // count
+    me = lax.axis_index("rows")
+    side = me % 2
+    other = me + 1 - 2 * side
     decays = forget * (1.0 - 0.2 * restart.astype(jnp.float32))
-    partial_value = jnp.einsum(
-        "srv,srw->svw", jacobian, jacobian, preferred_element_type=jnp.float32
-    )
-    gradient = jnp.einsum("sr,srv->sv", rhs, jacobian, preferred_element_type=jnp.float32)
-    both = jnp.concatenate([partial_value, gradient[:, None, :]], axis=1)
-    both = lax.psum(both, "rows")
-    local, retained = [both[0]], [decays[0]]
-    for s in range(1, segments_here):
-        local.append(decays[s] * local[-1] + both[s])
-        retained.append(decays[s] * retained[-1])
-    count, mine = lax.axis_size("tm"), lax.axis_index("tm")
-    ends = lax.all_gather(local[-1], "tm")
-    keeps = lax.all_gather(retained[-1], "tm")
-    before = jnp.zeros_like(local[0])
-    for t in range(count - 1):
-        before = jnp.where(t < mine, keeps[t] * before + ends[t], before)
-    post = jnp.stack([retained[s] * before + local[s] for s in range(segments_here)])
-    return smooth(post[:, :state_width], post[:, state_width], row_start, row_share)
+    parts = gram(decays, jacobian, rhs, count)
+    flat = exchange(decays, parts, count, steps).reshape(-1, LANES)
+    both = smooth(flat, width, me * row_share, other * row_share, row_share)
+    swap = [(k, k + 1 - 2 * (k % 2)) for k in range(count)]
+    here, there = both[0], lax.ppermute(both[1], "rows", swap)
+    pair = jnp.where(side == 0, jnp.stack([here, there]), jnp.stack([there, here]))
+    state = lax.dynamic_slice_in_dim(pair[:, row_share, :], me * row_share, row_share, 1)
+    return pair[:, :row_share, :], state
 
 
 def solution(mesh):

time: 198 us -> 78.7 us (0.40)
  the two profiles are of different devices: /device:TPU:0 before, /device:TPU:30 now
where the time goes in v2:
time: 78.7 us; the launch traced here: 78.5 us
  Pallas kernels  67.6 us (86%)
  waiting for transfers between devices  6.12 us (8%)
  local copies, waits for them, and re-layouts  3.2 us (4%)
    pallas_call x1, Pallas kernels, exchange(): pl.pallas_call(functools.partial(exchange_kernel, count, steps), out_shap...  46.8 us
    pallas_call x1, Pallas kernels, smooth(): pl.pallas_call(smoother_kernel, out_shape=jax.ShapeDtypeStruct((2, row_sh...  19.7 us
    ppermute x1, waiting for transfers between devices, on_device(): here, there = (both[0], lax.ppermute(both[1], 'rows', swap))  6.12 us
    unnamed x4, local copies, waits for them, and re-layouts  1.81 us
  transfers between devices with their start and end apart: 1, of which 1 were waited for; matrix products, arithmetic and copies ran while one was open for 0% of the time, Pallas kernels for 0%

profile of v2, /device:TPU:30, one launch (start us, length us, event | category | flops | bytes accessed | tf_op | source)
XLA Modules:
  0.0 78.5 jit_solution(3755623765062351388)
XLA Ops:
  0.6 0.7 subtract_multiply_fusion.decay_ref
  1.3 0.0 copy-start
  1.3 1.1 %copy-done = bf16[2,384,512]{2,1,0:T(8,128)(2,1)S(1)} copy-done((bf16[2,384,512]{2,1,0:T(8,128)(2,1)S(1)}, bf16[2,384,512]{2,1,0:T(8,128)(2,1)}, u32[]{:S(2)}) %copy-start) | copy-done | bytes 786456
  2.5 0.0 copy-start.1
  2.5 0.7 copy-done.1
  3.1 1.2 %shard_map.59.part_ref = f32[8,2,168,128]{3,2,1,0:T(8,128)S(1)} custom-call(f32[2]{0:T(128)S(1)} %subtract_multiply_fusion.decay_ref, bf16[2,384,512]{2,1,0:T(8,128)(2,1)S(1)} %copy-done, bf16[2,384]{1,0:T(2,128)(2,1)S(1)} %copy-done.1), custom_call_target="tpu_custom_call" | custom-call | tf_op jit(solution)/shard_map/pallas_call | solution.py:138
  4.3 46.8 %shard_map.60 = f32[8,168,128]{2,1,0:T(8,128)S(1)} custom-call(f32[2]{0:T(128)S(1)} %subtract_multiply_fusion.decay_ref, f32[8,2,168,128]{3,2,1,0:T(8,128)S(1)} %shard_map.59.part_ref), custom_call_target="tpu_custom_call" | custom-call | tf_op jit(solution)/shard_map/pallas_call | solution.py:246
  51.1 0.1 pad_add_fusion.place_ref
  51.2 19.7 %shard_map.61 = f32[2,72,512]{2,1,0:T(8,128)S(1)} custom-call(s32[2]{0:T(128)S(1)} %pad_add_fusion.place_ref, f32[1344,128]{1,0:T(8,128)S(1)} %bitcast.7), custom_call_target="tpu_custom_call" | custom-call | flops 268435456 | bytes 2097152 | tf_op jit(solution)/shard_map/pallas_call | solution.py:329
  70.9 0.1 collective-permute-start
  71.0 6.1 %collective-permute-done = f32[72,512]{1,0:T(8,128)S(1)} collective-permute-done((f32[72,512]{1,0:T(8,128)S(1)}, f32[72,512]{1,0:T(8,128)S(1)}, u32[]{:S(2)}, u32[]{:S(2)}) %collective-permute-start) | collective-permute-done | bytes 147488 | tf_op jit(solution)/shard_map/ppermute | solution.py:358
  77.1 0.7 slice.18
  77.9 0.6 constant_dynamic-slice_fusion
  (3 shorter events, 0.1 us)
Async XLA Ops:
  1.3 1.1 %copy-start = (bf16[2,384,512]{2,1,0:T(8,128)(2,1)S(1)}, bf16[2,384,512]{2,1,0:T(8,128)(2,1)}, u32[]{:S(2)}) copy-start(bf16[2,384,512]{2,1,0:T(8,128)(2,1)} %jac_ref.1) | copy-start | bytes 2359300
  2.5 0.7 copy-start.1
  70.9 6.2 %collective-permute-start = (f32[72,512]{1,0:T(8,128)S(1)}, f32[72,512]{1,0:T(8,128)S(1)}, u32[]{:S(2)}, u32[]{:S(2)}) collective-permute-start(f32[72,512]{1,0:T(8,128)S(1)} %get-tuple-element.3), channel_id=1, source_target_pairs={{0,4},{4,0},{8,12},{12,8},{16,20},{20,16},{24,28},{28,24},{1,5},{5... | collective-permute-start | bytes 442376 | tf_op jit(solution)/shard_map/ppermute | solution.py:358

commit v3 on v2

v3 whole, which is shorter than its diff:
```python
import functools

import jax
import jax.numpy as jnp
from jax import lax
from jax.experimental import pallas as pl
from jax.experimental.pallas import tpu as pltpu
from jax.sharding import PartitionSpec as P

HIGHEST = lax.Precision.HIGHEST
LANES = 128
GROUP = 8


def dot(a, b, over_a, over_b):
    return lax.dot_general(
        a, b, (((over_a,), (over_b,)), ((), ())),
        precision=HIGHEST, preferred_element_type=jnp.float32,
    )


def lane_spread(tile, lane):
    return jnp.broadcast_to(tile[:, lane : lane + 1], tile.shape)


def row_spread(tile, row):
    return jnp.broadcast_to(tile[row : row + 1, :], tile.shape)


def factor_tiles(many):
    lane = lax.broadcasted_iota(jnp.int32, (GROUP, LANES), 1)
    sub = lax.broadcasted_iota(jnp.int32, (GROUP, LANES), 0)
    many = [list(tiles) for tiles in many]
    count = len(many[0])
    here = range(len(many))
    over = [jnp.ones((GROUP, LANES), jnp.float32) for _ in here]
    pivots = [[None] * count for _ in here]
    for g in range(count):
        top = [many[s][g] for s in here]
        cols = [[lane_spread(top[s], g * GROUP + k) for k in range(GROUP)] for s in here]
        inverse = [[None] * GROUP for _ in here]
        rows = [[None] * GROUP for _ in here]
        heads = [[None] * GROUP for _ in here]
        for k in range(GROUP):
            at = g * GROUP + k
            for s in here:
                head = [None] * (k + 1) + [row_spread(c, k) for c in cols[s][k + 1 :]]
                pivot = row_spread(cols[s][k], k)
                inv = 1.0 / pivot
                times = jnp.where(sub > k, cols[s][k] * inv, 0.0)
                row = row_spread(top[s], k)
                row = jnp.where(lane == at, row + row, row)
                top[s] = top[s] - times * row
                for later in range(k + 1, GROUP):
                    cols[s][later] = cols[s][later] - times * head[later]
                inverse[s][k], rows[s][k], heads[s][k] = inv, row, head
                over[s] = jnp.where(lane == at, inv, over[s])
                pivots[s][g] = pivot if k == 0 else jnp.where(sub >= k, pivot, pivots[s][g])
        for s in here:
            many[s][g] = top[s]
        for v in range(g + 1, count):
            for s in here:
                tile = many[s][v]
                mine = [lane_spread(tile, g * GROUP + k) for k in range(GROUP)]
                for k in range(GROUP):
                    times = mine[k] * inverse[s][k]
                    tile = tile - times * rows[s][k]
                    for later in range(k + 1, GROUP):
                        mine[later] = mine[later] - times * heads[s][k][later]
                many[s][v] = tile
    upper, lower = [], []
    for s in here:
        ups, lows = [], []
        for g in range(count):
            scale = lax.rsqrt(pivots[s][g])
            tile = many[s][g] * scale
            at = sub + g * GROUP
            ups.append(jnp.where(lane >= at, tile, 0.0))
            lows.append(jnp.where(lane <= at, tile * over[s], 0.0))
        upper.append(ups)
        lower.append(lows)
    return upper, lower


EARLY = ((0, 1, True), (0, 1, False), (0, 2, False), (0, 3, False))
LATE = ((1, 2, False), (1, 3, False), (2, 3, False), (2, 3, True))


def shard_rows(count):
    part = len(EARLY) * LANES // count
    return part, part + GROUP, 2 * part + GROUP


def gram_kernel(decay_ref, jac_ref, rhs_ref, out_ref):
    count = out_ref.shape[0]
    part, early, _ = shard_rows(count)
    width = jac_ref.shape[2]
    blocks = width // LANES
    keep = decay_ref[1]
    lane = lax.broadcasted_iota(jnp.int32, (LANES, LANES), 1)
    sub = lax.broadcasted_iota(jnp.int32, (LANES, LANES), 0)
    tiles = [{}, {}]
    for i in range(blocks):
        lo, hi = i * LANES, (i + 1) * LANES
        first, second = [
            lax.dot_general(
                jac_ref[s, :, lo:hi], jac_ref[s, :, lo:], (((0,), (0,)), ((), ())),
                preferred_element_type=jnp.float32,
            )
            for s in range(2)
        ]
        second = keep * first + second
        for j in range(i, blocks):
            left = (j - i) * LANES
            tiles[0][i, j] = first[:, left : left + LANES]
            tiles[1][i, j] = second[:, left : left + LANES]
    vecs = [
        jnp.dot(rhs_ref[s : s + 1, :], jac_ref[s], preferred_element_type=jnp.float32) for s in range(2)
    ]
    vecs[1] = keep * vecs[0] + vecs[1]
    for s in range(2):
        for names, base in ((EARLY, 0), (LATE, early)):
            for q, (i, j, square) in enumerate(names):
                tile = tiles[s][i, j]
                if square:
                    tile = jnp.where(lane > sub, tiles[s][i, i], tiles[s][j, j])
                for k in range(count // len(names)):
                    out_ref[q * (count // len(names)) + k, s, base : base + part, :] = tile[k * part : (k + 1) * part, :]
        extra = [vecs[s][:, lo : lo + LANES] for lo in range(0, width, LANES)]
        for i in (0, 2):
            extra.append(jnp.sum(jnp.where(lane == sub, tiles[s][i, i], 0.0), axis=0, keepdims=True))
        extra.append(jnp.zeros((GROUP - len(extra), LANES), jnp.float32))
        out_ref[0, s, part:early, :] = jnp.concatenate(extra, axis=0)
        for owner in range(1, count):
            out_ref[owner, s, part:early, :] = jnp.zeros((GROUP, LANES), jnp.float32)


def gram(decays, jacobian, rhs, count):
    vmem = pl.BlockSpec(memory_space=pltpu.VMEM)
    return pl.pallas_call(
        gram_kernel,
        out_shape=jax.ShapeDtypeStruct((count, 2, shard_rows(count)[2], LANES), jnp.float32),
        in_specs=[pl.BlockSpec(memory_space=pltpu.SMEM), vmem, vmem],
        out_specs=vmem,
        compiler_params=pltpu.CompilerParams(vmem_limit_bytes=40 * 1024 * 1024),
    )(decays, jacobian, rhs)


def smooth_kernel(
    count, steps, decay_ref, part_ref, rows_ref, state_ref,
    near, far, mine, past, post, prior, weight, front, back, work, inv, vec,
    near_send, near_recv, far_send, far_recv, past_send, past_recv,
    front_send, front_recv, back_send, back_recv, swap_send, swap_recv,
):
    me, now = lax.axis_index("rows"), lax.axis_index("tm")
    half = count // 2
    part, early, share = shard_rows(count)
    other_row = me + 1 - 2 * (me % 2)
    line, side = me // 2, me % 2

    barrier = pltpu.get_barrier_semaphore()
    for j in range(1, count):
        pl.semaphore_signal(
            barrier, inc=1, device_id=((me + j) % count, now), device_id_type=pl.DeviceIdType.MESH
        )
    for j in range(1, steps):
        pl.semaphore_signal(
            barrier, inc=1, device_id=(me, (now + j) % steps), device_id_type=pl.DeviceIdType.MESH
        )
    pl.semaphore_wait(barrier, count + steps - 2)

    def send(src, dst, send_sem, recv_sem, row, step):
        return pltpu.make_async_remote_copy(
            src_ref=src, dst_ref=dst, send_sem=send_sem, recv_sem=recv_sem,
            device_id=(row, step), device_id_type=pl.DeviceIdType.MESH,
        )

    order = list(range(1, half)) + [0]
    first = {}
    for j in order:
        owner = 2 * ((line + j) % half) + (1 - side)
        first[j] = send(
            part_ref.at[owner], near.at[j], near_send.at[j], near_recv.at[j], 2 * line + (1 - side), now
        )
        first[j].start()
    second = {}
    for j in order:
        first[j].wait_recv()
        owner = 2 * ((line + j) % half) + side
        near[j] = near[j] + part_ref[owner]
        if j:
            second[j] = send(near.at[j], far.at[j], far_send.at[j], far_recv.at[j], owner, now)
            second[j].start()
    total = near[0]
    for j in range(1, half):
        second[j].wait_recv()
        total = total + far[j]
    keep0, keep1 = decay_ref[0], decay_ref[1]
    mine[:, :share, :] = total
    mine[:, share:, :] = jnp.full((2, GROUP, LANES), keep0 * keep1, jnp.float32)

    passed = {}
    for j in range(1, steps):
        passed[j] = send(
            mine.at[1], past.at[j], past_send.at[j], past_recv.at[j], me, (now + j) % steps
        )

        @pl.when(now + j < steps)
        def _(j=j):
            passed[j].start()

    prior[...] = jnp.zeros_like(prior)
    weight[...] = jnp.ones_like(weight)
    for j in range(1, steps):
        @pl.when(now >= j)
        def _(j=j):
            passed[j].wait_recv()
            prior[...] = prior[...] + weight[0:1, :] * past[j, :share, :]
            weight[...] = weight[...] * past[j, share:, :]

    post[0] = keep0 * prior[...] + mine[0, :share, :]
    post[1] = (keep0 * keep1) * prior[...] + mine[1, :share, :]

    first_part, last_part = {}, {}
    for j in range(1, count):
        other = (me + j) % count
        first_part[j] = send(
            post.at[other % 2, pl.ds(0, early)], front.at[me], front_send.at[j], front_recv.at[j], other, now
        )
        last_part[j] = send(
            post.at[other % 2, pl.ds(early, part)], back.at[me], back_send.at[j], back_recv.at[j], other, now
        )
    for j in range(1, count):
        first_part[j].start()
    front[me] = post[side, 0:early]
    back[me] = post[side, early:]
    for j in range(1, count):
        first_part[j].wait_recv()
    for j in range(1, count):
        last_part[j].start()

    width = work.shape[1]
    blocks = width // LANES
    tiles = LANES // GROUP
    lane = lax.broadcasted_iota(jnp.int32, (LANES, LANES), 1)
    sub = lax.broadcasted_iota(jnp.int32, (LANES, LANES), 0)

    def unpack(names, source):
        every = count // len(names)
        for q, (i, j, square) in enumerate(names):
            tile = jnp.concatenate([source[q * every + k, :part, :] for k in range(every)], axis=0)
            if square:
                diagonal = front[0, part + blocks + i // 2 : part + blocks + i // 2 + 1, :]
                over = jnp.where(lane > sub, tile, 0.0)
                under = jnp.where(lane < sub, tile, 0.0)
                work[i * LANES : (i + 1) * LANES, i * LANES : (i + 1) * LANES] = (
                    over + over.T + jnp.where(lane == sub, diagonal, 0.0)
                )
                work[j * LANES : (j + 1) * LANES, j * LANES : (j + 1) * LANES] = tile - over + under.T
            else:
                work[i * LANES : (i + 1) * LANES, j * LANES : (j + 1) * LANES] = tile

    unpack(EARLY, front)
    for j in range(blocks):
        vec[:, j * LANES : (j + 1) * LANES] = jnp.broadcast_to(
            front[0, part + j : part + j + 1, :], (GROUP, LANES)
        )
    row_share = rows_ref.shape[1]
    swap = send(
        work.at[pl.ds(pl.multiple_of(other_row * row_share, GROUP), row_share)],
        rows_ref.at[side], swap_send.at[0], swap_recv.at[0], other_row, now,
    )
    swap_state = send(
        vec, state_ref.at[side], swap_send.at[1], swap_recv.at[1], other_row, now
    )

    def block_step(b, carry):
        base = pl.multiple_of(b * LANES, LANES)

        def place(t):
            return pl.ds(pl.multiple_of(base + t * GROUP, GROUP), GROUP)

        upper, lower = factor_tiles([[work[place(t), pl.ds(base, LANES)] for t in range(tiles)]])
        for t in range(tiles):
            work[place(t), pl.ds(base, LANES)] = upper[0][t]
            inv[place(t), :] = lower[0][t]

        for i in range(blocks):
            @pl.when(b == i)
            def _(i=i):
                lo, hi = i * LANES, (i + 1) * LANES
                low = inv[lo:hi, :]
                y = dot(vec[:, lo:hi], low, 1, 1)
                vec[:, lo:hi] = y
                if i < blocks - 1:
                    panel = dot(low, work[lo:hi, hi:], 1, 0)
                    work[lo:hi, hi:] = panel
                    vec[:, hi:] = vec[:, hi:] - dot(y, panel, 1, 0)
                    if i == 0:
                        for j in range(1, count):
                            last_part[j].wait_recv()
                        unpack(LATE, back)
                    for j in range(i + 1, blocks):
                        left = (j - i - 1) * LANES
                        jl, jh = j * LANES, (j + 1) * LANES
                        work[jl:jh, jl:] = work[jl:jh, jl:] - dot(
                            panel[:, left : left + LANES], panel[:, left:], 0, 0
                        )
                        work[jl:jh, lo:hi] = jnp.zeros((LANES, LANES), jnp.float32)

        @pl.when((me * row_share) // LANES == b)
        def _():
            swap.start()

        return carry

    lax.fori_loop(0, blocks, block_step, 0)
    for b in reversed(range(blocks)):
        lo, hi = b * LANES, (b + 1) * LANES
        right = vec[:, lo:hi]
        if b < blocks - 1:
            right = right - dot(vec[:, hi:], work[lo:hi, hi:], 1, 1)
        vec[:, lo:hi] = dot(right, inv[lo:hi, :], 1, 0)
    swap_state.start()
    rows_ref[side] = work[pl.ds(pl.multiple_of(me * row_share, GROUP), row_share), :]
    state_ref[side] = vec[...]

    for j in order:
        first[j].wait_send()
        if j:
            second[j].wait_send()
    for j in range(1, steps):
        @pl.when(now + j < steps)
        def _(j=j):
            passed[j].wait_send()
    for j in range(1, count):
        first_part[j].wait_send()
        last_part[j].wait_send()
    swap.wait()
    swap_state.wait()


def smooth(decays, parts, width, count, steps):
    part, early, share = shard_rows(count)
    half = count // 2
    vmem = pl.BlockSpec(memory_space=pltpu.VMEM)
    dma = pltpu.SemaphoreType.DMA
    f32 = jnp.float32
    return pl.pallas_call(
        functools.partial(smooth_kernel, count, steps),
        out_shape=(
            jax.ShapeDtypeStruct((2, width // count, width), f32),
            jax.ShapeDtypeStruct((2, GROUP, width), f32),
        ),
        in_specs=[pl.BlockSpec(memory_space=pltpu.SMEM), vmem],
        out_specs=(vmem, vmem),
        scratch_shapes=[
            pltpu.VMEM((half, 2, share, LANES), f32),
            pltpu.VMEM((half, 2, share, LANES), f32),
            pltpu.VMEM((2, share + GROUP, LANES), f32),
            pltpu.VMEM((steps, share + GROUP, LANES), f32),
            pltpu.VMEM((2, share, LANES), f32),
            pltpu.VMEM((share, LANES), f32),
            pltpu.VMEM((GROUP, LANES), f32),
            pltpu.VMEM((count, early, LANES), f32),
            pltpu.VMEM((count, part, LANES), f32),
            pltpu.VMEM((width, width), f32),
            pltpu.VMEM((width, LANES), f32),
            pltpu.VMEM((GROUP, width), f32),
            dma((half,)), dma((half,)), dma((half,)), dma((half,)),
            dma((steps,)), dma((steps,)), dma((count,)), dma((count,)),
            dma((count,)), dma((count,)), dma((2,)), dma((2,)),
        ],
        compiler_params=pltpu.CompilerParams(
            collective_id=0, has_side_effects=True, vmem_limit_bytes=40 * 1024 * 1024
        ),
    )(decays, parts)


def on_device(jacobian, rhs, forget, restart):
    width = jacobian.shape[2]
    count, steps = lax.axis_size("rows"), lax.axis_size("tm")
    row_share = width // count
    decays = forget * (1.0 - 0.2 * restart.astype(jnp.float32))
    parts = gram(decays, jacobian, rhs, count)
    factor, state = smooth(decays, parts, width, count, steps)
    start = lax.axis_index("rows") * row_share
    return factor, lax.dynamic_slice_in_dim(state[:, 0, :], start, row_share, 1)


def solution(mesh):
    in_specs = (P("tm", "rows", None), P("tm", "rows"), P("tm"), P("tm"))
    out_specs = (P("tm", "rows", None), P("tm", "rows"))
    return jax.shard_map(
        on_device, mesh=mesh, in_specs=in_specs, out_specs=out_specs, check_vma=False
    )
```

time: 78.7 us -> 66.6 us (0.85)
  the two profiles are of different devices: /device:TPU:30 before, /device:TPU:5 now
where the time goes in v3:
time: 66.6 us; the launch traced here: 66.4 us
  Pallas kernels  61.9 us (93%)
  local copies, waits for them, and re-layouts  3.16 us (5%)
  other arithmetic  0.68 us (1%)
    pallas_call x1, Pallas kernels, smooth(): pl.pallas_call(functools.partial(smooth_kernel, count, steps), out_shape=...  60.7 us
    unnamed x5, local copies, waits for them, and re-layouts  2.51 us

profile of v3, /device:TPU:5, one launch (start us, length us, event | category | flops | bytes accessed | tf_op | source)
XLA Modules:
  0.0 66.4 jit_solution(570996558089362706)
XLA Ops:
  0.6 0.7 %subtract_multiply_fusion.decay_ref = f32[2]{0:T(128)S(1)} fusion(f32[2]{0:T(128)} %param.6, s32[2]{0:T(128)} %param.7), kind=kLoop, calls=%fused_computation | loop fusion | flops 8 | bytes 24 | tf_op jit(solution)/shard_map/mul | solution.py:384
  1.3 0.0 copy-start
  1.3 1.1 %copy-done = bf16[2,384,512]{2,1,0:T(8,128)(2,1)S(1)} copy-done((bf16[2,384,512]{2,1,0:T(8,128)(2,1)S(1)}, bf16[2,384,512]{2,1,0:T(8,128)(2,1)}, u32[]{:S(2)}) %copy-start) | copy-done | bytes 786456
  2.4 0.0 copy-start.1
  2.4 0.7 %copy-done.1 = bf16[2,384]{1,0:T(2,128)(2,1)S(1)} copy-done((bf16[2,384]{1,0:T(2,128)(2,1)S(1)}, bf16[2,384]{1,0:T(2,128)(2,1)}, u32[]{:S(2)}) %copy-start.1) | copy-done | bytes 1560
  3.1 1.2 %shard_map.59.part_ref = f32[8,2,136,128]{3,2,1,0:T(8,128)S(1)} custom-call(f32[2]{0:T(128)S(1)} %subtract_multiply_fusion.decay_ref, bf16[2,384,512]{2,1,0:T(8,128)(2,1)S(1)} %copy-done, bf16[2,384]{1,0:T(2,128)(2,1)S(1)} %copy-done.1), custom_call_target="tpu_custom_call" | custom-call | tf_op jit(solution)/shard_map/pallas_call | solution.py:140
  4.3 60.7 %shard_map.60 = (f32[2,64,512]{2,1,0:T(8,128)S(1)}, f32[2,8,512]{2,1,0:T(8,128)S(1)}) custom-call(f32[2]{0:T(128)S(1)} %subtract_multiply_fusion.decay_ref, f32[8,2,136,128]{3,2,1,0:T(8,128)S(1)} %shard_map.59.part_ref), custom_call_target="tpu_custom_call" | custom-call | tf_op jit(solution)/shard_map/pallas_call | solution.py:349
  65.1 0.6 constant_dynamic-slice_fusion
  65.7 0.7 %copy.7 = f32[2,64,512]{2,1,0:T(8,128)} copy(f32[2,64,512]{2,1,0:T(8,128)S(1)} %get-tuple-element.8) | data formatting | bytes 524288
  (1 shorter events, 0.0 us)
Async XLA Ops:
  1.3 1.1 %copy-start = (bf16[2,384,512]{2,1,0:T(8,128)(2,1)S(1)}, bf16[2,384,512]{2,1,0:T(8,128)(2,1)}, u32[]{:S(2)}) copy-start(bf16[2,384,512]{2,1,0:T(8,128)(2,1)} %jac_ref.1) | copy-start | bytes 2359300
  2.4 0.7 %copy-start.1 = (bf16[2,384]{1,0:T(2,128)(2,1)S(1)}, bf16[2,384]{1,0:T(2,128)(2,1)}, u32[]{:S(2)}) copy-start(bf16[2,384]{1,0:T(2,128)(2,1)} %rhs_ref.1) | copy-start | bytes 4612

commit v4 on v3

v4 whole, which is shorter than its diff:
```python
import functools

import jax
import jax.numpy as jnp
from jax import lax
from jax.experimental import pallas as pl
from jax.experimental.pallas import tpu as pltpu
from jax.sharding import PartitionSpec as P

HIGHEST = lax.Precision.HIGHEST
LANES = 128
GROUP = 8


def dot(a, b, over_a, over_b):
    return lax.dot_general(
        a, b, (((over_a,), (over_b,)), ((), ())),
        precision=HIGHEST, preferred_element_type=jnp.float32,
    )


def lane_spread(tile, lane):
    return jnp.broadcast_to(tile[:, lane : lane + 1], tile.shape)


def row_spread(tile, row):
    return jnp.broadcast_to(tile[row : row + 1, :], tile.shape)


def factor_tiles(many):
    lane = lax.broadcasted_iota(jnp.int32, (GROUP, LANES), 1)
    sub = lax.broadcasted_iota(jnp.int32, (GROUP, LANES), 0)
    many = [list(tiles) for tiles in many]
    count = len(many[0])
    here = range(len(many))
    over = [jnp.ones((GROUP, LANES), jnp.float32) for _ in here]
    pivots = [[None] * count for _ in here]
    for g in range(count):
        top = [many[s][g] for s in here]
        cols = [[lane_spread(top[s], g * GROUP + k) for k in range(GROUP)] for s in here]
        inverse = [[None] * GROUP for _ in here]
        rows = [[None] * GROUP for _ in here]
        heads = [[None] * GROUP for _ in here]
        for k in range(GROUP):
            at = g * GROUP + k
            for s in here:
                head = [None] * (k + 1) + [row_spread(c, k) for c in cols[s][k + 1 :]]
                pivot = row_spread(cols[s][k], k)
                inv = 1.0 / pivot
                times = jnp.where(sub > k, cols[s][k] * inv, 0.0)
                row = row_spread(top[s], k)
                row = jnp.where(lane == at, row + row, row)
                top[s] = top[s] - times * row
                for later in range(k + 1, GROUP):
                    cols[s][later] = cols[s][later] - times * head[later]
                inverse[s][k], rows[s][k], heads[s][k] = inv, row, head
                over[s] = jnp.where(lane == at, inv, over[s])
                pivots[s][g] = pivot if k == 0 else jnp.where(sub >= k, pivot, pivots[s][g])
        for s in here:
            many[s][g] = top[s]
        for v in range(g + 1, count):
            for s in here:
                tile = many[s][v]
                mine = [lane_spread(tile, g * GROUP + k) for k in range(GROUP)]
                for k in range(GROUP):
                    times = mine[k] * inverse[s][k]
                    tile = tile - times * rows[s][k]
                    for later in range(k + 1, GROUP):
                        mine[later] = mine[later] - times * heads[s][k][later]
                many[s][v] = tile
    upper, lower = [], []
    for s in here:
        ups, lows = [], []
        for g in range(count):
            scale = lax.rsqrt(pivots[s][g])
            tile = many[s][g] * scale
            at = sub + g * GROUP
            ups.append(jnp.where(lane >= at, tile, 0.0))
            lows.append(jnp.where(lane <= at, tile * over[s], 0.0))
        upper.append(ups)
        lower.append(lows)
    return upper, lower


EARLY = ((0, 1, True), (0, 1, False), (0, 2, False), (0, 3, False))
LATE = ((1, 2, False), (1, 3, False), (2, 3, False), (2, 3, True))


def shard_rows(count):
    part = len(EARLY) * LANES // count
    return part, part + GROUP, 2 * part + GROUP


def smooth_kernel(count, steps, forget_ref, restart_ref, jac_ref, rhs_ref, rows_ref, state_ref, *scratch):
    chunks = (scratch[:16], scratch[16:32])
    weight, work, inv, vec, swap_send, swap_recv = scratch[32:]
    me, now = lax.axis_index("rows"), lax.axis_index("tm")
    half = count // 2
    part, early, share = shard_rows(count)
    line, side = me // 2, me % 2
    other_row = me + 1 - 2 * side
    keep0, keep1 = [forget_ref[k] * (1.0 - 0.2 * restart_ref[k].astype(jnp.float32)) for k in range(2)]
    lane = lax.broadcasted_iota(jnp.int32, (LANES, LANES), 1)
    sub = lax.broadcasted_iota(jnp.int32, (LANES, LANES), 0)

    barrier = pltpu.get_barrier_semaphore()
    for j in range(1, count):
        pl.semaphore_signal(
            barrier, inc=1, device_id=((me + j) % count, now), device_id_type=pl.DeviceIdType.MESH
        )
    for j in range(1, steps):
        pl.semaphore_signal(
            barrier, inc=1, device_id=(me, (now + j) % steps), device_id_type=pl.DeviceIdType.MESH
        )

    def send(src, dst, send_sem, recv_sem, row, step):
        return pltpu.make_async_remote_copy(
            src_ref=src, dst_ref=dst, send_sem=send_sem, recv_sem=recv_sem,
            device_id=(row, step), device_id_type=pl.DeviceIdType.MESH,
        )

    width = jac_ref.shape[2]
    blocks = width // LANES
    tiles = [{}, {}]

    def gram(i):
        lo, hi = i * LANES, (i + 1) * LANES
        first, second = [
            lax.dot_general(
                jac_ref[s, :, lo:hi], jac_ref[s, :, lo:], (((0,), (0,)), ((), ())),
                preferred_element_type=jnp.float32,
            )
            for s in range(2)
        ]
        second = keep1 * first + second
        for j in range(i, blocks):
            left = (j - i) * LANES
            tiles[0][i, j] = first[:, left : left + LANES]
            tiles[1][i, j] = second[:, left : left + LANES]

    def pack(names, part_ref):
        every = count // len(names)
        for s in range(2):
            for q, (i, j, square) in enumerate(names):
                tile = tiles[s][i, j]
                if square:
                    tile = jnp.where(lane > sub, tiles[s][i, i], tiles[s][j, j])
                for k in range(every):
                    part_ref[q * every + k, s, :part, :] = tile[k * part : (k + 1) * part, :]

    def pack_vectors(part_ref):
        vecs = [
            jnp.dot(rhs_ref[s : s + 1, :], jac_ref[s], preferred_element_type=jnp.float32) for s in range(2)
        ]
        vecs[1] = keep1 * vecs[0] + vecs[1]
        for s in range(2):
            extra = [vecs[s][:, lo : lo + LANES] for lo in range(0, width, LANES)]
            extra.append(jnp.sum(jnp.where(lane == sub, tiles[s][0, 0], 0.0), axis=0, keepdims=True))
            extra.append(jnp.sum(jnp.where(lane == sub, tiles[s][2, 2], 0.0), axis=0, keepdims=True))
            extra.append(jnp.zeros((GROUP - len(extra), LANES), jnp.float32))
            part_ref[0, s, part:, :] = jnp.concatenate(extra, axis=0)
            for owner in range(1, count):
                part_ref[owner, s, part:, :] = jnp.zeros((GROUP, LANES), jnp.float32)

    order = list(range(1, half)) + [0]
    first, second, passed, last = [({}, {}) for _ in range(4)]

    def pair_start(c):
        part_ref, near, near_send, near_recv = (chunks[c][0], chunks[c][1], chunks[c][8], chunks[c][9])
        for j in order:
            owner = 2 * ((line + j) % half) + (1 - side)
            first[c][j] = send(
                part_ref.at[owner], near.at[j], near_send.at[j], near_recv.at[j], other_row, now
            )
            first[c][j].start()

    def pair_finish(c, places):
        part_ref, near, far, far_send, far_recv = chunks[c][:3] + chunks[c][10:12]
        for j in places:
            first[c][j].wait_recv()
            owner = 2 * ((line + j) % half) + side
            near[j] = near[j] + part_ref[owner]
            if j:
                second[c][j] = send(near.at[j], far.at[j], far_send.at[j], far_recv.at[j], owner, now)
                second[c][j].start()

    def pass_on(c):
        near, far, mine, past, past_send, past_recv = chunks[c][1:5] + chunks[c][12:14]
        total = near[0]
        for j in range(1, half):
            second[c][j].wait_recv()
            total = total + far[j]
        size = total.shape[1]
        mine[:, :size, :] = total
        mine[:, size:, :] = jnp.full((2, GROUP, LANES), keep0 * keep1, jnp.float32)
        for j in range(1, steps):
            passed[c][j] = send(
                mine.at[1], past.at[j], past_send.at[j], past_recv.at[j], me, (now + j) % steps
            )

            @pl.when(now + j < steps)
            def _(j=j):
                passed[c][j].start()

    def spread(c):
        mine, past, post, prior, whole, last_send, last_recv = chunks[c][3:8] + chunks[c][14:16]
        size = post.shape[1]
        prior[...] = jnp.zeros_like(prior)
        weight[...] = jnp.ones_like(weight)
        for j in range(1, steps):
            @pl.when(now >= j)
            def _(j=j):
                passed[c][j].wait_recv()
                prior[...] = prior[...] + weight[0:1, :] * past[j, :size, :]
                weight[...] = weight[...] * past[j, size:, :]

        post[0] = keep0 * prior[...] + mine[0, :size, :]
        post[1] = (keep0 * keep1) * prior[...] + mine[1, :size, :]
        for j in range(1, count):
            other = (me + j) % count
            last[c][j] = send(
                post.at[other % 2], whole.at[me], last_send.at[j], last_recv.at[j], other, now
            )
            last[c][j].start()
        whole[me] = post[side]

    gram(0)
    gram(1)
    pack(EARLY, chunks[0][0])
    gram(2)
    pack_vectors(chunks[0][0])
    pl.semaphore_wait(barrier, count + steps - 2)
    pair_start(0)
    gram(3)
    pack(LATE, chunks[1][0])
    pair_start(1)
    pair_finish(0, order)
    pair_finish(1, order[: half // 2])
    pass_on(0)
    pair_finish(1, order[half // 2 :])
    spread(0)
    pass_on(1)
    spread(1)
    front, back = chunks[0][7], chunks[1][7]
    for j in range(1, count):
        last[0][j].wait_recv()

    tiles = LANES // GROUP

    def unpack(names, source):
        every = count // len(names)
        for q, (i, j, square) in enumerate(names):
            tile = jnp.concatenate([source[q * every + k, :part, :] for k in range(every)], axis=0)
            if square:
                diagonal = front[0, part + blocks + i // 2 : part + blocks + i // 2 + 1, :]
                over = jnp.where(lane > sub, tile, 0.0)
                under = jnp.where(lane < sub, tile, 0.0)
                work[i * LANES : (i + 1) * LANES, i * LANES : (i + 1) * LANES] = (
                    over + over.T + jnp.where(lane == sub, diagonal, 0.0)
                )
                work[j * LANES : (j + 1) * LANES, j * LANES : (j + 1) * LANES] = tile - over + under.T
            else:
                work[i * LANES : (i + 1) * LANES, j * LANES : (j + 1) * LANES] = tile

    unpack(EARLY, front)
    for j in range(blocks):
        vec[:, j * LANES : (j + 1) * LANES] = jnp.broadcast_to(
            front[0, part + j : part + j + 1, :], (GROUP, LANES)
        )
    row_share = rows_ref.shape[1]
    swap = send(
        work.at[pl.ds(pl.multiple_of(other_row * row_share, GROUP), row_share)],
        rows_ref.at[side], swap_send.at[0], swap_recv.at[0], other_row, now,
    )
    swap_state = send(
        vec, state_ref.at[side], swap_send.at[1], swap_recv.at[1], other_row, now
    )

    def block_step(b, carry):
        base = pl.multiple_of(b * LANES, LANES)

        def place(t):
            return pl.ds(pl.multiple_of(base + t * GROUP, GROUP), GROUP)

        upper, lower = factor_tiles([[work[place(t), pl.ds(base, LANES)] for t in range(tiles)]])
        for t in range(tiles):
            work[place(t), pl.ds(base, LANES)] = upper[0][t]
            inv[place(t), :] = lower[0][t]

        for i in range(blocks):
            @pl.when(b == i)
            def _(i=i):
                lo, hi = i * LANES, (i + 1) * LANES
                low = inv[lo:hi, :]
                y = dot(vec[:, lo:hi], low, 1, 1)
                vec[:, lo:hi] = y
                if i < blocks - 1:
                    panel = dot(low, work[lo:hi, hi:], 1, 0)
                    work[lo:hi, hi:] = panel
                    vec[:, hi:] = vec[:, hi:] - dot(y, panel, 1, 0)
                    if i == 0:
                        for j in range(1, count):
                            last[1][j].wait_recv()
                        unpack(LATE, back)
                    for j in range(i + 1, blocks):
                        left = (j - i - 1) * LANES
                        jl, jh = j * LANES, (j + 1) * LANES
                        work[jl:jh, jl:] = work[jl:jh, jl:] - dot(
                            panel[:, left : left + LANES], panel[:, left:], 0, 0
                        )
                        work[jl:jh, lo:hi] = jnp.zeros((LANES, LANES), jnp.float32)

        @pl.when((me * row_share) // LANES == b)
        def _():
            swap.start()

        return carry

    lax.fori_loop(0, blocks, block_step, 0)
    for b in reversed(range(blocks)):
        lo, hi = b * LANES, (b + 1) * LANES
        right = vec[:, lo:hi]
        if b < blocks - 1:
            right = right - dot(vec[:, hi:], work[lo:hi, hi:], 1, 1)
        vec[:, lo:hi] = dot(right, inv[lo:hi, :], 1, 0)
    swap_state.start()
    rows_ref[side] = work[pl.ds(pl.multiple_of(me * row_share, GROUP), row_share), :]
    state_ref[side] = vec[...]

    for c in range(2):
        for j in order:
            first[c][j].wait_send()
            if j:
                second[c][j].wait_send()
        for j in range(1, steps):
            @pl.when(now + j < steps)
            def _(j=j):
                passed[c][j].wait_send()
        for j in range(1, count):
            last[c][j].wait_send()
    swap.wait()
    swap_state.wait()


def smooth(forget, restart, jacobian, rhs, count, steps):
    width = jacobian.shape[2]
    part, early, _ = shard_rows(count)
    half = count // 2
    vmem = pl.BlockSpec(memory_space=pltpu.VMEM)
    smem = pl.BlockSpec(memory_space=pltpu.SMEM)
    dma = pltpu.SemaphoreType.DMA
    f32 = jnp.float32
    scratch = []
    for size in (early, part):
        scratch += [
            pltpu.VMEM((count, 2, size, LANES), f32),
            pltpu.VMEM((half, 2, size, LANES), f32),
            pltpu.VMEM((half, 2, size, LANES), f32),
            pltpu.VMEM((2, size + GROUP, LANES), f32),
            pltpu.VMEM((steps, size + GROUP, LANES), f32),
            pltpu.VMEM((2, size, LANES), f32),
            pltpu.VMEM((size, LANES), f32),
            pltpu.VMEM((count, size, LANES), f32),
            dma((half,)), dma((half,)), dma((half,)), dma((half,)),
            dma((steps,)), dma((steps,)), dma((count,)), dma((count,)),
        ]
    scratch += [
        pltpu.VMEM((GROUP, LANES), f32),
        pltpu.VMEM((width, width), f32),
        pltpu.VMEM((width, LANES), f32),
        pltpu.VMEM((GROUP, width), f32),
        dma((2,)), dma((2,)),
    ]
    return pl.pallas_call(
        functools.partial(smooth_kernel, count, steps),
        out_shape=(
            jax.ShapeDtypeStruct((2, width // count, width), f32),
            jax.ShapeDtypeStruct((2, GROUP, width), f32),
        ),
        in_specs=[smem, smem, vmem, vmem],
        out_specs=(vmem, vmem),
        scratch_shapes=scratch,
        compiler_params=pltpu.CompilerParams(
            collective_id=0, has_side_effects=True, vmem_limit_bytes=40 * 1024 * 1024
        ),
    )(forget, restart, jacobian, rhs)


def on_device(jacobian, rhs, forget, restart):
    count, steps = lax.axis_size("rows"), lax.axis_size("tm")
    row_share = jacobian.shape[2] // count
    factor, state = smooth(forget, restart, jacobian, rhs, count, steps)
    start = lax.axis_index("rows") * row_share
    return factor, lax.dynamic_slice_in_dim(state[:, 0, :], start, row_share, 1)


def solution(mesh):
    in_specs = (P("tm", "rows", None), P("tm", "rows"), P("tm"), P("tm"))
    out_specs = (P("tm", "rows", None), P("tm", "rows"))
    return jax.shard_map(
        on_device, mesh=mesh, in_specs=in_specs, out_specs=out_specs, check_vma=False
    )
```

time: 66.6 us -> 59.3 us (0.89)
  the two profiles are of different devices: /device:TPU:5 before, /device:TPU:0 now
where the time goes in v4:
time: 59.3 us; the launch traced here: 59.2 us
  Pallas kernels  55.3 us (93%)
  local copies, waits for them, and re-layouts  3.14 us (5%)
  between operations  0.68 us (1%)
    pallas_call x1, Pallas kernels, smooth(): pl.pallas_call(functools.partial(smooth_kernel, count, steps), out_shape=...  55.3 us
    unnamed x9, local copies, waits for them, and re-layouts  2.5 us

profile of v4, /device:TPU:0, one launch (start us, length us, event | category | flops | bytes accessed | tf_op | source)
XLA Modules:
  0.0 59.2 jit_solution(16828565340780590151)
XLA Ops:
  0.6 0.0 copy-start.1
  0.6 0.0 copy-start.2
  0.7 0.0 copy-start.3
  0.7 0.7 %copy-done.1 = bf16[2,384]{1,0:T(2,128)(2,1)S(1)} copy-done((bf16[2,384]{1,0:T(2,128)(2,1)S(1)}, bf16[2,384]{1,0:T(2,128)(2,1)}, u32[]{:S(2)}) %copy-start.1) | copy-done | bytes 1560
  1.3 0.0 copy-done.2
  1.3 0.0 copy-done.3
  1.3 0.0 copy-start
  1.3 1.1 %copy-done = bf16[2,384,512]{2,1,0:T(8,128)(2,1)S(1)} copy-done((bf16[2,384,512]{2,1,0:T(8,128)(2,1)S(1)}, bf16[2,384,512]{2,1,0:T(8,128)(2,1)}, u32[]{:S(2)}) %copy-start) | copy-done | bytes 786456
  2.5 55.3 %shard_map.59 = (f32[2,64,512]{2,1,0:T(8,128)S(1)}, f32[2,8,512]{2,1,0:T(8,128)S(1)}) custom-call(f32[2]{0:T(128)S(1)} %copy-done.2, s32[2]{0:T(128)S(1)} %copy-done.3, bf16[2,384,512]{2,1,0:T(8,128)(2,1)S(1)} %copy-done, bf16[2,384]{1,0:T(2,128)(2,1)S(1)} %copy-done.1), custom_call_target="tpu_custom_call" | custom-call | tf_op jit(solution)/shard_map/pallas_call | solution.py:374
  57.8 0.6 %constant_dynamic-slice_fusion = f32[2,1,64]{2,1,0:T(1,128)} fusion(f32[2,1,512]{2,1,0:T(1,128)S(1)} %slice.3, s32[]{:T(128)S(6)} %select_n.3), kind=kLoop, calls=%fused_computation | loop fusion | bytes 1028 | tf_op jit(solution)/shard_map/dynamic_slice | solution.py:394
  58.5 0.7 %copy.7 = f32[2,64,512]{2,1,0:T(8,128)} copy(f32[2,64,512]{2,1,0:T(8,128)S(1)} %get-tuple-element.8) | data formatting | bytes 524288
  (1 shorter events, 0.0 us)
Async XLA Ops:
  0.6 0.7 %copy-start.1 = (bf16[2,384]{1,0:T(2,128)(2,1)S(1)}, bf16[2,384]{1,0:T(2,128)(2,1)}, u32[]{:S(2)}) copy-start(bf16[2,384]{1,0:T(2,128)(2,1)} %rhs_ref.1) | copy-start | bytes 4612
  0.6 0.7 %copy-start.2 = (f32[2]{0:T(128)S(1)}, f32[2]{0:T(128)}, u32[]{:S(2)}) copy-start(f32[2]{0:T(128)} %forget_ref.1) | copy-start | bytes 28
  0.7 0.7 %copy-start.3 = (s32[2]{0:T(128)S(1)}, s32[2]{0:T(128)}, u32[]{:S(2)}) copy-start(s32[2]{0:T(128)} %restart_ref.1) | copy-start | bytes 28
  1.3 1.1 %copy-start = (bf16[2,384,512]{2,1,0:T(8,128)(2,1)S(1)}, bf16[2,384,512]{2,1,0:T(8,128)(2,1)}, u32[]{:S(2)}) copy-start(bf16[2,384,512]{2,1,0:T(8,128)(2,1)} %jac_ref.1) | copy-start | bytes 2359300

commit v5 on v4

--- a/solution.py
+++ b/solution.py
@@ -93,12 +93,19 @@
 
 def smooth_kernel(count, steps, forget_ref, restart_ref, jac_ref, rhs_ref, rows_ref, state_ref, *scratch):
     chunks = (scratch[:16], scratch[16:32])
-    weight, work, inv, vec, swap_send, swap_recv = scratch[32:]
+    weight, work, inv, vec, rows_send, rows_recv, state_send, state_recv = scratch[32:]
     me, now = lax.axis_index("rows"), lax.axis_index("tm")
     half = count // 2
     part, early, share = shard_rows(count)
     line, side = me // 2, me % 2
     other_row = me + 1 - 2 * side
+
+    def inner(row):
+        return jnp.logical_or((row // 2) % 4 == 1, (row // 2) % 4 == 2)
+
+    factors = inner(me)
+    guest = 2 * jnp.where(line % 4 == 1, line - 1, jnp.minimum(line + 1, half - 1))
+    takers = (other_row, guest, guest + 1)
     keep0, keep1 = [forget_ref[k] * (1.0 - 0.2 * restart_ref[k].astype(jnp.float32)) for k in range(2)]
     lane = lax.broadcasted_iota(jnp.int32, (LANES, LANES), 1)
     sub = lax.broadcasted_iota(jnp.int32, (LANES, LANES), 0)
@@ -221,7 +228,11 @@
             last[c][j] = send(
                 post.at[other % 2], whole.at[me], last_send.at[j], last_recv.at[j], other, now
             )
-            last[c][j].start()
+
+            @pl.when(inner(other))
+            def _(j=j):
+                last[c][j].start()
+
         whole[me] = post[side]
 
     gram(0)
@@ -242,9 +253,6 @@
     pass_on(1)
     spread(1)
     front, back = chunks[0][7], chunks[1][7]
-    for j in range(1, count):
-        last[0][j].wait_recv()
-
     tiles = LANES // GROUP
 
     def unpack(names, source):
@@ -262,70 +270,110 @@
             else:
                 work[i * LANES : (i + 1) * LANES, j * LANES : (j + 1) * LANES] = tile
 
-    unpack(EARLY, front)
-    for j in range(blocks):
-        vec[:, j * LANES : (j + 1) * LANES] = jnp.broadcast_to(
-            front[0, part + j : part + j + 1, :], (GROUP, LANES)
+    row_share = rows_ref.shape[1]
+
+    def rows_to(k, i):
+        start = pl.multiple_of(takers[k] * row_share, GROUP)
+        return send(
+            work.at[pl.ds(start, row_share), pl.ds(i * LANES, width - i * LANES)],
+            rows_ref.at[side, :, pl.ds(i * LANES, width - i * LANES)],
+            rows_send.at[k], rows_recv.at[side], takers[k], now,
         )
-    row_share = rows_ref.shape[1]
-    swap = send(
-        work.at[pl.ds(pl.multiple_of(other_row * row_share, GROUP), row_share)],
-        rows_ref.at[side], swap_send.at[0], swap_recv.at[0], other_row, now,
-    )
-    swap_state = send(
-        vec, state_ref.at[side], swap_send.at[1], swap_recv.at[1], other_row, now
-    )
-
-    def block_step(b, carry):
-        base = pl.multiple_of(b * LANES, LANES)
-
-        def place(t):
-            return pl.ds(pl.multiple_of(base + t * GROUP, GROUP), GROUP)
-
-        upper, lower = factor_tiles([[work[place(t), pl.ds(base, LANES)] for t in range(tiles)]])
-        for t in range(tiles):
-            work[place(t), pl.ds(base, LANES)] = upper[0][t]
-            inv[place(t), :] = lower[0][t]
-
+
+    def state_to(k):
+        return send(vec, state_ref.at[side], state_send.at[k], state_recv.at[side], takers[k], now)
+
+    def give_rows(i):
+        for k in range(3):
+            @pl.when((takers[k] * row_share) // LANES == i)
+            def _(k=k):
+                rows_to(k, i).start()
+
+    for i in range(1, blocks):
+        @pl.when((me * row_share) // LANES == i)
+        def _(i=i):
+            rows_ref[:, :, : i * LANES] = jnp.zeros((2, row_share, i * LANES), jnp.float32)
+
+    @pl.when(factors)
+    def _():
+        for j in range(1, count):
+            last[0][j].wait_recv()
+        unpack(EARLY, front)
+        for j in range(blocks):
+            vec[:, j * LANES : (j + 1) * LANES] = jnp.broadcast_to(
+                front[0, part + j : part + j + 1, :], (GROUP, LANES)
+            )
+
+        def block_step(b, carry):
+            base = pl.multiple_of(b * LANES, LANES)
+
+            def place(t):
+                return pl.ds(pl.multiple_of(base + t * GROUP, GROUP), GROUP)
+
+            upper, lower = factor_tiles([[work[place(t), pl.ds(base, LANES)] for t in range(tiles)]])
+            for t in range(tiles):
+                work[place(t), pl.ds(base, LANES)] = upper[0][t]
+                inv[place(t), :] = lower[0][t]
+
+            for i in range(blocks):
+                @pl.when(b == i)
+                def _(i=i):
+                    lo, hi = i * LANES, (i + 1) * LANES
+                    low = inv[lo:hi, :]
+                    y = dot(vec[:, lo:hi], low, 1, 1)
+                    vec[:, lo:hi] = y
+                    if i < blocks - 1:
+                        panel = dot(low, work[lo:hi, hi:], 1, 0)
+                        work[lo:hi, hi:] = panel
+                        vec[:, hi:] = vec[:, hi:] - dot(y, panel, 1, 0)
+                    give_rows(i)
+                    if i < blocks - 1:
+                        if i == 0:
+                            for j in range(1, count):
+                                last[1][j].wait_recv()
+                            unpack(LATE, back)
+                        for j in range(i + 1, blocks):
+                            left = (j - i - 1) * LANES
+                            jl, jh = j * LANES, (j + 1) * LANES
+                            work[jl:jh, jl:] = work[jl:jh, jl:] - dot(
+                                panel[:, left : left + LANES], panel[:, left:], 0, 0
+                            )
+                            work[jl:jh, lo:hi] = jnp.zeros((LANES, LANES), jnp.float32)
+
+            return carry
+
+        lax.fori_loop(0, blocks, block_step, 0)
+        for b in reversed(range(blocks)):
+            lo, hi = b * LANES, (b + 1) * LANES
+            right = vec[:, lo:hi]
+            if b < blocks - 1:
+                right = right - dot(vec[:, hi:], work[lo:hi, hi:], 1, 1)
+            vec[:, lo:hi] = dot(right, inv[lo:hi, :], 1, 0)
+        for k in range(3):
+            state_to(k).start()
         for i in range(blocks):
-            @pl.when(b == i)
+            @pl.when((me * row_share) // LANES == i)
             def _(i=i):
-                lo, hi = i * LANES, (i + 1) * LANES
-                low = inv[lo:hi, :]
-                y = dot(vec[:, lo:hi], low, 1, 1)
-                vec[:, lo:hi] = y
-                if i < blocks - 1:
-                    panel = dot(low, work[lo:hi, hi:], 1, 0)
-                    work[lo:hi, hi:] = panel
-                    vec[:, hi:] = vec[:, hi:] - dot(y, panel, 1, 0)
-                    if i == 0:
-                        for j in range(1, count):
-                            last[1][j].wait_recv()
-                        unpack(LATE, back)
-                    for j in range(i + 1, blocks):
-                        left = (j - i - 1) * LANES
-                        jl, jh = j * LANES, (j + 1) * LANES
-                        work[jl:jh, jl:] = work[jl:jh, jl:] - dot(
-                            panel[:, left : left + LANES], panel[:, left:], 0, 0
-                        )
-                        work[jl:jh, lo:hi] = jnp.zeros((LANES, LANES), jnp.float32)
-
-        @pl.when((me * row_share) // LANES == b)
-        def _():
-            swap.start()
-
-        return carry
-
-    lax.fori_loop(0, blocks, block_step, 0)
-    for b in reversed(range(blocks)):
-        lo, hi = b * LANES, (b + 1) * LANES
-        right = vec[:, lo:hi]
-        if b < blocks - 1:
-            right = right - dot(vec[:, hi:], work[lo:hi, hi:], 1, 1)
-        vec[:, lo:hi] = dot(right, inv[lo:hi, :], 1, 0)
-    swap_state.start()
-    rows_ref[side] = work[pl.ds(pl.multiple_of(me * row_share, GROUP), row_share), :]
-    state_ref[side] = vec[...]
+                start = pl.multiple_of(me * row_share, GROUP)
+                rows_ref[side, :, i * LANES :] = work[pl.ds(start, row_share), i * LANES :]
+        state_ref[side] = vec[...]
+        for k in range(3):
+            for i in range(blocks):
+                @pl.when((takers[k] * row_share) // LANES == i)
+                def _(k=k, i=i):
+                    rows_to(k, i).wait_send()
+            state_to(k).wait_send()
+
+    for s in range(2):
+        @pl.when(jnp.logical_or(jnp.logical_not(factors), side != s))
+        def _(s=s):
+            for i in range(blocks):
+                @pl.when((me * row_share) // LANES == i)
+                def _(i=i):
+                    kept = rows_ref.at[s, :, pl.ds(i * LANES, width - i * LANES)]
+                    send(kept, kept, rows_send.at[0], rows_recv.at[s], other_row, now).wait_recv()
+            kept = state_ref.at[s]
+            send(kept, kept, state_send.at[0], state_recv.at[s], other_row, now).wait_recv()
 
     for c in range(2):
         for j in order:
@@ -337,9 +385,9 @@
             def _(j=j):
                 passed[c][j].wait_send()
         for j in range(1, count):
-            last[c][j].wait_send()
-    swap.wait()
-    swap_state.wait()
+            @pl.when(inner((me + j) % count))
+            def _(j=j):
+                last[c][j].wait_send()
 
 
 def smooth(forget, restart, jacobian, rhs, count, steps):
@@ -369,7 +417,7 @@
         pltpu.VMEM((width, width), f32),
         pltpu.VMEM((width, LANES), f32),
         pltpu.VMEM((GROUP, width), f32),
-        dma((2,)), dma((2,)),
+        dma((3,)), dma((2,)), dma((3,)), dma((2,)),
     ]
     return pl.pallas_call(
         functools.partial(smooth_kernel, count, steps),

time: 59.3 us -> 57.2 us (0.965)
  Pallas kernels: 55.3 us -> 53.2 us
    pallas_call x1, Pallas kernels: 55.3 us -> 53.2 us  [smooth(): pl.pallas_call(functools.partial(smooth_kernel, count, steps), out_shape=...]
where the time goes in v5:
time: 57.2 us; the launch traced here: 57 us
  Pallas kernels  53.2 us (93%)
  local copies, waits for them, and re-layouts  3.14 us (5%)
  between operations  0.68 us (1%)
    pallas_call x1, Pallas kernels, smooth(): pl.pallas_call(functools.partial(smooth_kernel, count, steps), out_shape=...  53.2 us
    unnamed x9, local copies, waits for them, and re-layouts  2.5 us

profile of v5, /device:TPU:0, one launch (start us, length us, event | category | flops | bytes accessed | tf_op | source)
XLA Modules:
  0.0 57.0 jit_solution(6736537883354799717)
XLA Ops:
  0.6 0.0 copy-start.1
  0.6 0.0 copy-start.2
  0.7 0.0 copy-start.3
  0.7 0.7 %copy-done.1 = bf16[2,384]{1,0:T(2,128)(2,1)S(1)} copy-done((bf16[2,384]{1,0:T(2,128)(2,1)S(1)}, bf16[2,384]{1,0:T(2,128)(2,1)}, u32[]{:S(2)}) %copy-start.1) | copy-done | bytes 1560
  1.3 0.0 copy-done.2
  1.3 0.0 copy-done.3
  1.3 0.0 copy-start
  1.3 1.1 %copy-done = bf16[2,384,512]{2,1,0:T(8,128)(2,1)S(1)} copy-done((bf16[2,384,512]{2,1,0:T(8,128)(2,1)S(1)}, bf16[2,384,512]{2,1,0:T(8,128)(2,1)}, u32[]{:S(2)}) %copy-start) | copy-done | bytes 786456
  2.5 53.2 %shard_map.59 = (f32[2,64,512]{2,1,0:T(8,128)S(1)}, f32[2,8,512]{2,1,0:T(8,128)S(1)}) custom-call(f32[2]{0:T(128)S(1)} %copy-done.2, s32[2]{0:T(128)S(1)} %copy-done.3, bf16[2,384,512]{2,1,0:T(8,128)(2,1)S(1)} %copy-done, bf16[2,384]{1,0:T(2,128)(2,1)S(1)} %copy-done.1), custom_call_target="tpu_custom_call" | custom-call | tf_op jit(solution)/shard_map/pallas_call | solution.py:422
  55.7 0.6 %constant_dynamic-slice_fusion = f32[2,1,64]{2,1,0:T(1,128)} fusion(f32[2,1,512]{2,1,0:T(1,128)S(1)} %slice.3, s32[]{:T(128)S(6)} %select_n.3), kind=kLoop, calls=%fused_computation | loop fusion | bytes 1028 | tf_op jit(solution)/shard_map/dynamic_slice | solution.py:442
  56.3 0.7 %copy.7 = f32[2,64,512]{2,1,0:T(8,128)} copy(f32[2,64,512]{2,1,0:T(8,128)S(1)} %get-tuple-element.8) | data formatting | bytes 524288
  (1 shorter events, 0.0 us)
Async XLA Ops:
  0.6 0.7 %copy-start.1 = (bf16[2,384]{1,0:T(2,128)(2,1)S(1)}, bf16[2,384]{1,0:T(2,128)(2,1)}, u32[]{:S(2)}) copy-start(bf16[2,384]{1,0:T(2,128)(2,1)} %rhs_ref.1) | copy-start | bytes 4612
  0.6 0.7 %copy-start.2 = (f32[2]{0:T(128)S(1)}, f32[2]{0:T(128)}, u32[]{:S(2)}) copy-start(f32[2]{0:T(128)} %forget_ref.1) | copy-start | bytes 28
  0.7 0.7 %copy-start.3 = (s32[2]{0:T(128)S(1)}, s32[2]{0:T(128)}, u32[]{:S(2)}) copy-start(s32[2]{0:T(128)} %restart_ref.1) | copy-start | bytes 28
  1.3 1.1 %copy-start = (bf16[2,384,512]{2,1,0:T(8,128)(2,1)S(1)}, bf16[2,384,512]{2,1,0:T(8,128)(2,1)}, u32[]{:S(2)}) copy-start(bf16[2,384,512]{2,1,0:T(8,128)(2,1)} %jac_ref.1) | copy-start | bytes 2359300

commit v6 on v5

--- a/solution.py
+++ b/solution.py
@@ -41,12 +41,19 @@
         inverse = [[None] * GROUP for _ in here]
         rows = [[None] * GROUP for _ in here]
         heads = [[None] * GROUP for _ in here]
+        square = [
+            {(i, k): row_spread(cols[s][k], i) for k in range(GROUP) for i in range(k, GROUP)} for s in here
+        ]
         for k in range(GROUP):
             at = g * GROUP + k
             for s in here:
-                head = [None] * (k + 1) + [row_spread(c, k) for c in cols[s][k + 1 :]]
-                pivot = row_spread(cols[s][k], k)
+                head = [None] * (k + 1) + [square[s][i, k] for i in range(k + 1, GROUP)]
+                pivot = square[s][k, k]
                 inv = 1.0 / pivot
+                for i in range(k + 1, GROUP):
+                    share = square[s][i, k] * inv
+                    for j in range(k + 1, i + 1):
+                        square[s][i, j] = square[s][i, j] - share * square[s][j, k]
                 times = jnp.where(sub > k, cols[s][k] * inv, 0.0)
                 row = row_spread(top[s], k)
                 row = jnp.where(lane == at, row + row, row)

time: 57.2 us -> 58.1 us (1.016)
  Pallas kernels: 53.2 us -> 54.1 us
    pallas_call x1, Pallas kernels: 53.2 us -> 54.1 us  [smooth(): pl.pallas_call(functools.partial(smooth_kernel, count, steps), out_shape=...]
where the time goes in v6:
time: 58.1 us; the launch traced here: 57.9 us
  Pallas kernels  54.1 us (93%)
  local copies, waits for them, and re-layouts  3.14 us (5%)
  between operations  0.68 us (1%)
    pallas_call x1, Pallas kernels, smooth(): pl.pallas_call(functools.partial(smooth_kernel, count, steps), out_shape=...  54.1 us
    unnamed x9, local copies, waits for them, and re-layouts  2.5 us

profile of v6, /device:TPU:0, one launch (start us, length us, event | category | flops | bytes accessed | tf_op | source)
XLA Modules:
  0.0 57.9 jit_solution(6605645324287123409)
XLA Ops:
  0.6 0.0 copy-start.1
  0.6 0.0 copy-start.2
  0.7 0.0 copy-start.3
  0.7 0.7 %copy-done.1 = bf16[2,384]{1,0:T(2,128)(2,1)S(1)} copy-done((bf16[2,384]{1,0:T(2,128)(2,1)S(1)}, bf16[2,384]{1,0:T(2,128)(2,1)}, u32[]{:S(2)}) %copy-start.1) | copy-done | bytes 1560
  1.3 0.0 copy-done.2
  1.3 0.0 copy-done.3
  1.3 0.0 copy-start
  1.3 1.1 %copy-done = bf16[2,384,512]{2,1,0:T(8,128)(2,1)S(1)} copy-done((bf16[2,384,512]{2,1,0:T(8,128)(2,1)S(1)}, bf16[2,384,512]{2,1,0:T(8,128)(2,1)}, u32[]{:S(2)}) %copy-start) | copy-done | bytes 786456
  2.5 54.1 %shard_map.59 = (f32[2,64,512]{2,1,0:T(8,128)S(1)}, f32[2,8,512]{2,1,0:T(8,128)S(1)}) custom-call(f32[2]{0:T(128)S(1)} %copy-done.2, s32[2]{0:T(128)S(1)} %copy-done.3, bf16[2,384,512]{2,1,0:T(8,128)(2,1)S(1)} %copy-done, bf16[2,384]{1,0:T(2,128)(2,1)S(1)} %copy-done.1), custom_call_target="tpu_custom_call" | custom-call | tf_op jit(solution)/shard_map/pallas_call | solution.py:429
  56.5 0.6 %constant_dynamic-slice_fusion = f32[2,1,64]{2,1,0:T(1,128)} fusion(f32[2,1,512]{2,1,0:T(1,128)S(1)} %slice.3, s32[]{:T(128)S(6)} %select_n.3), kind=kLoop, calls=%fused_computation | loop fusion | bytes 1028 | tf_op jit(solution)/shard_map/dynamic_slice | solution.py:449
  57.2 0.7 %copy.7 = f32[2,64,512]{2,1,0:T(8,128)} copy(f32[2,64,512]{2,1,0:T(8,128)S(1)} %get-tuple-element.8) | data formatting | bytes 524288
  (1 shorter events, 0.0 us)
Async XLA Ops:
  0.6 0.7 %copy-start.1 = (bf16[2,384]{1,0:T(2,128)(2,1)S(1)}, bf16[2,384]{1,0:T(2,128)(2,1)}, u32[]{:S(2)}) copy-start(bf16[2,384]{1,0:T(2,128)(2,1)} %rhs_ref.1) | copy-start | bytes 4612
  0.6 0.7 %copy-start.2 = (f32[2]{0:T(128)S(1)}, f32[2]{0:T(128)}, u32[]{:S(2)}) copy-start(f32[2]{0:T(128)} %forget_ref.1) | copy-start | bytes 28
  0.7 0.7 %copy-start.3 = (s32[2]{0:T(128)S(1)}, s32[2]{0:T(128)}, u32[]{:S(2)}) copy-start(s32[2]{0:T(128)} %restart_ref.1) | copy-start | bytes 28
  1.3 1.1 %copy-start = (bf16[2,384,512]{2,1,0:T(8,128)(2,1)S(1)}, bf16[2,384,512]{2,1,0:T(8,128)(2,1)}, u32[]{:S(2)}) copy-start(bf16[2,384,512]{2,1,0:T(8,128)(2,1)} %jac_ref.1) | copy-start | bytes 2359300

commit v7 on v5

--- a/solution.py
+++ b/solution.py
@@ -58,7 +58,20 @@
                 pivots[s][g] = pivot if k == 0 else jnp.where(sub >= k, pivot, pivots[s][g])
         for s in here:
             many[s][g] = top[s]
-        for v in range(g + 1, count):
+        turned = []
+        for s in here:
+            scaled = top[s] * inverse[s][0]
+            for k in range(1, GROUP):
+                scaled = jnp.where(sub >= k, top[s] * inverse[s][k], scaled)
+            turned.append(scaled.T)
+        for v in range(g + 2, count):
+            for s in here:
+                tile = many[s][v]
+                for k in range(GROUP):
+                    times = turned[s][v * GROUP : (v + 1) * GROUP, k : k + 1]
+                    tile = tile - jnp.broadcast_to(times, tile.shape) * rows[s][k]
+                many[s][v] = tile
+        for v in range(g + 1, min(g + 2, count)):
             for s in here:
                 tile = many[s][v]
                 mine = [lane_spread(tile, g * GROUP + k) for k in range(GROUP)]

time: 57.2 us -> 64 us (1.12)
  Pallas kernels: 53.2 us -> 60 us
    pallas_call x1, Pallas kernels: 53.2 us -> 60 us  [smooth(): pl.pallas_call(functools.partial(smooth_kernel, count, steps), out_shape=...]
where the time goes in v7:
time: 64 us; the launch traced here: 63.8 us
  Pallas kernels  60 us (94%)
  local copies, waits for them, and re-layouts  3.14 us (5%)
  between operations  0.68 us (1%)
    pallas_call x1, Pallas kernels, smooth(): pl.pallas_call(functools.partial(smooth_kernel, count, steps), out_shape=...  60 us
    unnamed x9, local copies, waits for them, and re-layouts  2.5 us

profile of v7, /device:TPU:0, one launch (start us, length us, event | category | flops | bytes accessed | tf_op | source)
XLA Modules:
  0.0 63.8 jit_solution(7960530041385985634)
XLA Ops:
  0.6 0.0 copy-start.1
  0.6 0.0 copy-start.2
  0.7 0.0 copy-start.3
  0.7 0.7 %copy-done.1 = bf16[2,384]{1,0:T(2,128)(2,1)S(1)} copy-done((bf16[2,384]{1,0:T(2,128)(2,1)S(1)}, bf16[2,384]{1,0:T(2,128)(2,1)}, u32[]{:S(2)}) %copy-start.1) | copy-done | bytes 1560
  1.3 0.0 copy-done.2
  1.3 0.0 copy-done.3
  1.3 0.0 copy-start
  1.3 1.1 %copy-done = bf16[2,384,512]{2,1,0:T(8,128)(2,1)S(1)} copy-done((bf16[2,384,512]{2,1,0:T(8,128)(2,1)S(1)}, bf16[2,384,512]{2,1,0:T(8,128)(2,1)}, u32[]{:S(2)}) %copy-start) | copy-done | bytes 786456
  2.5 60.0 %shard_map.59 = (f32[2,64,512]{2,1,0:T(8,128)S(1)}, f32[2,8,512]{2,1,0:T(8,128)S(1)}) custom-call(f32[2]{0:T(128)S(1)} %copy-done.2, s32[2]{0:T(128)S(1)} %copy-done.3, bf16[2,384,512]{2,1,0:T(8,128)(2,1)S(1)} %copy-done, bf16[2,384]{1,0:T(2,128)(2,1)S(1)} %copy-done.1), custom_call_target="tpu_custom_call" | custom-call | tf_op jit(solution)/shard_map/pallas_call | solution.py:435
  62.4 0.6 %constant_dynamic-slice_fusion = f32[2,1,64]{2,1,0:T(1,128)} fusion(f32[2,1,512]{2,1,0:T(1,128)S(1)} %slice.3, s32[]{:T(128)S(6)} %select_n.3), kind=kLoop, calls=%fused_computation | loop fusion | bytes 1028 | tf_op jit(solution)/shard_map/dynamic_slice | solution.py:455
  63.1 0.7 %copy.7 = f32[2,64,512]{2,1,0:T(8,128)} copy(f32[2,64,512]{2,1,0:T(8,128)S(1)} %get-tuple-element.8) | data formatting | bytes 524288
  (1 shorter events, 0.0 us)
Async XLA Ops:
  0.6 0.7 %copy-start.1 = (bf16[2,384]{1,0:T(2,128)(2,1)S(1)}, bf16[2,384]{1,0:T(2,128)(2,1)}, u32[]{:S(2)}) copy-start(bf16[2,384]{1,0:T(2,128)(2,1)} %rhs_ref.1) | copy-start | bytes 4612
  0.6 0.7 %copy-start.2 = (f32[2]{0:T(128)S(1)}, f32[2]{0:T(128)}, u32[]{:S(2)}) copy-start(f32[2]{0:T(128)} %forget_ref.1) | copy-start | bytes 28
  0.7 0.7 %copy-start.3 = (s32[2]{0:T(128)S(1)}, s32[2]{0:T(128)}, u32[]{:S(2)}) copy-start(s32[2]{0:T(128)} %restart_ref.1) | copy-start | bytes 28
  1.3 1.1 %copy-start = (bf16[2,384,512]{2,1,0:T(8,128)(2,1)S(1)}, bf16[2,384,512]{2,1,0:T(8,128)(2,1)}, u32[]{:S(2)}) copy-start(bf16[2,384,512]{2,1,0:T(8,128)(2,1)} %jac_ref.1) | copy-start | bytes 2359300
